TPU v7x, 256 devices: a whole 4x4x8 slice. The times are simulated.
256 devices in a mesh: seq: 32 (over x_hi, z, core), head: 8 (over x_lo, y).
Axes of the slice: x: 4 (x_hi: 2, x_lo: 2; x = x_hi * 2 + x_lo), y: 4, z: 8, core: 2. Of those that a mesh axis runs over, the one named last changes fastest.
Arguments:
- signal: bfloat16 [32768, 2048], P('seq', 'head'), may hold values from -6 to 6
- write_keys: bfloat16 [32768, 128], P('seq'), may hold values from -1.5 to 1.5
- read_queries: bfloat16 [32768, 128], P('seq'), may hold values from -1.5 to 1.5
- step_sizes: float32 [32, 32768], P('head', 'seq'), may hold values from 0.005 to 0.02
- log_decay: float32 [32, 32768], P('head', 'seq'), as said below
- mirror_heads: int32 [32], replicated, may hold values from 0 to 31, each once
- contig_starts: int32 [4], replicated, may hold values from 1 to 32767
- out_grad: bfloat16 [32768, 2048], P('seq', 'head'), may hold values from -6 to 6
Outputs:
- signal_grad: float32 [32768, 2048], P('seq', 'head')
- write_grad: float32 [32768, 128], P('seq')
- read_grad: float32 [32768, 128], P('seq')
- step_grad: float32 [32, 32768], P('head', 'seq')
- decay_grad: float32 [32, 32768], P('head', 'seq')
Inputs may be any that keep to these rules, and one draw needn't show every extreme that they name: `mirror_heads`: a permutation of the 32 heads. `contig_starts`: start positions of contigs, in no particular order, repeats possible. `log_decay`: every entry is negative.
All inputs are finite; a program needn't handle non-finite values.
Results may differ from a plain program's by a relative error of at most 0.0003.
Values sent between devices are 32-bit elements; how exact they have to be, the bound alone decides.
A program may use at most 128 MiB of HBM per device.

v0:
```python
import jax
import jax.numpy as jnp
from jax import lax
from jax.sharding import PartitionSpec as P

BLOCK = 256


highest = lax.Precision.HIGHEST


def shifted(value, axis, steps):
    count = lax.axis_size(axis)
    leading, last = (max(0, -steps), min(count, count - steps))
    return lax.ppermute(value, axis, [(source, source + steps) for source in range(leading, last)])


def block_step(carried_pair, block_data):
    state_in, seg_last = carried_pair
    values, write_rows, read_rows, step_rows, decays, segments = block_data
    cumulative = jnp.cumsum(decays, axis=1)
    places = jnp.arange(segments.shape[0])
    allowed = (places[:, None] >= places[None, :]) & (segments[:, None] == segments[None, :])
    log_gap = cumulative[:, :, None] - cumulative[:, None, :]
    decay_mat = jnp.where(allowed[None], jnp.exp(jnp.where(allowed[None], log_gap, 0.0)), 0.0)
    scores = jnp.dot(read_rows, write_rows.T, precision=highest)
    weights = decay_mat * scores[None] * step_rows[:, None, :]
    inside = jnp.einsum("hts,shp->thp", weights, values, precision=highest)
    entering = jnp.exp(cumulative) * (segments == seg_last).astype(cumulative.dtype)[None, :]
    carried = (
        jnp.einsum("tn,hpn->thp", read_rows, state_in, precision=highest) * entering.T[:, :, None]
    )
    leaving = (
        jnp.exp(cumulative[:, -1:] - cumulative)
        * (segments == segments[-1]).astype(cumulative.dtype)[None, :]
        * step_rows
    )
    written = jnp.einsum(
        "shp,sn->hpn", values * leaving.T[:, :, None], write_rows, precision=highest
    )
    new_state = state_in * entering[:, -1][:, None, None] + written
    return ((new_state, segments[-1]), inside + carried)


def strand(values, write_rows, read_rows, step_rows, decays, segments, seg_before, state_in):
    length, head_count, head_width = values.shape
    block_count = length // BLOCK
    state_dim = write_rows.shape[1]
    blocks = (
        values.reshape(block_count, BLOCK, head_count, head_width),
        write_rows.reshape(block_count, BLOCK, state_dim),
        read_rows.reshape(block_count, BLOCK, state_dim),
        step_rows.reshape(head_count, block_count, BLOCK).transpose(1, 0, 2),
        decays.reshape(head_count, block_count, BLOCK).transpose(1, 0, 2),
        segments.reshape(block_count, BLOCK),
    )
    finale, outputs = lax.scan(jax.checkpoint(block_step), (state_in, seg_before), blocks)
    return (outputs.reshape(length, head_count, head_width), finale[0])


def boundary_terms(
    values, write_rows, read_rows, cotangent, step_rows, decays, segments, seg_before
):
    cumulative = jnp.cumsum(decays, axis=1)
    entering = jnp.exp(cumulative) * (segments == seg_before).astype(cumulative.dtype)[None, :]
    through = entering[:, -1]
    leaving = (
        jnp.exp(cumulative[:, -1:] - cumulative)
        * (segments == segments[-1]).astype(cumulative.dtype)[None, :]
        * step_rows
    )
    ending = jnp.einsum(
        "shp,sn->hpn", values * leaving.T[:, :, None], write_rows, precision=highest
    )
    incoming = jnp.einsum(
        "shp,sn->hpn", cotangent * entering.T[:, :, None], read_rows, precision=highest
    )
    return (through, ending, incoming)


def on_device(
    signal, write_keys, read_queries, step_sizes, log_decay, mirror_heads, contig_starts, out_grad
):
    length = signal.shape[0]
    local_heads = step_sizes.shape[0]
    head_width = signal.shape[1] // local_heads
    all_heads = mirror_heads.shape[0]
    values = signal.astype(jnp.float32).reshape(length, local_heads, head_width)
    cotangent = out_grad.astype(jnp.float32).reshape(length, local_heads, head_width)
    write_rows = write_keys.astype(jnp.float32)
    read_rows = read_queries.astype(jnp.float32)
    offset = lax.axis_index("seq") * length
    span_total = lax.axis_size("seq") * length
    token_positions = offset + jnp.arange(length, dtype=jnp.int32)
    segments = jnp.sum(contig_starts[None, :] <= token_positions[:, None], axis=1)
    seg_before = jnp.where(offset == 0, -1, jnp.sum(contig_starts <= offset - 1))
    seg_after = jnp.where(
        offset + length >= span_total, -1, jnp.sum(contig_starts <= offset + length)
    )
    steps_all, decays_all = (
        lax.all_gather(step_sizes, "head", axis=0, tiled=True),
        lax.all_gather(log_decay, "head", axis=0, tiled=True),
    )
    own_ids = lax.axis_index("head") * local_heads + jnp.arange(local_heads, dtype=jnp.int32)
    picked = (jnp.arange(all_heads, dtype=jnp.int32)[None, :] == own_ids[:, None]).astype(jnp.int32)
    partner = jnp.sum(picked * mirror_heads[None, :], axis=1)
    selector = (partner[:, None] == jnp.arange(all_heads, dtype=jnp.int32)[None, :]).astype(
        jnp.float32
    )
    mirror_steps = jnp.dot(selector, steps_all, precision=highest)
    mirror_decays = jnp.dot(selector, decays_all, precision=highest)
    front_gain, front_end, front_seed = boundary_terms(
        values, write_rows, read_rows, cotangent, step_sizes, log_decay, segments, seg_before
    )
    mirror_gain, mirror_end, mirror_seed = boundary_terms(
        values[::-1],
        write_rows[::-1],
        read_rows[::-1],
        cotangent[::-1],
        mirror_steps[:, ::-1],
        mirror_decays[:, ::-1],
        segments[::-1],
        seg_after,
    )
    upward = jnp.stack([front_end, mirror_seed])
    downward = jnp.stack([mirror_end, front_seed])
    up_gain = jnp.stack([front_gain, mirror_gain])
    down_gain = jnp.stack([mirror_gain, front_gain])

    def relay(step_index, carried_pair):
        rising, falling = carried_pair
        rising = shifted(up_gain[:, :, None, None] * rising + upward, "seq", 1)
        falling = shifted(down_gain[:, :, None, None] * falling + downward, "seq", -1)
        return (rising, falling)

    rising, falling = lax.fori_loop(
        0, lax.axis_size("seq") - 1, relay, (jnp.zeros_like(upward), jnp.zeros_like(downward))
    )
    front_state, mirror_adjoint = (rising[0], rising[1])
    mirror_state, front_adjoint = (falling[0], falling[1])

    def strands(values, write_rows, read_rows, step_rows, decays, other_steps, other_decays):
        front_out, front_final = strand(
            values, write_rows, read_rows, step_rows, decays, segments, seg_before, front_state
        )
        back_out, back_final = strand(
            values[::-1],
            write_rows[::-1],
            read_rows[::-1],
            other_steps[:, ::-1],
            other_decays[:, ::-1],
            segments[::-1],
            seg_after,
            mirror_state,
        )
        return (front_out + back_out[::-1], front_final, back_final)

    output, pullback = jax.vjp(
        strands, values, write_rows, read_rows, step_sizes, log_decay, mirror_steps, mirror_decays
    )
    gradients = pullback((cotangent, front_adjoint, mirror_adjoint))
    spread_steps = jnp.dot(selector.T, gradients[5], precision=highest)
    spread_decays = jnp.dot(selector.T, gradients[6], precision=highest)
    step_back, decay_back = (
        lax.psum_scatter(spread_steps, "head", scatter_dimension=0, tiled=True),
        lax.psum_scatter(spread_decays, "head", scatter_dimension=0, tiled=True),
    )
    write_grad, read_grad = lax.psum((gradients[1], gradients[2]), "head")
    signal_grad = gradients[0].reshape(length, local_heads * head_width)
    return (signal_grad, write_grad, read_grad, gradients[3] + step_back, gradients[4] + decay_back)


def solution(mesh):
    return jax.shard_map(
        on_device,
        mesh=mesh,
        in_specs=(
            P("seq", "head"),
            P("seq", None),
            P("seq", None),
            P("head", "seq"),
            P("head", "seq"),
            P(),
            P(),
            P("seq", "head"),
        ),
        out_specs=(
            P("seq", "head"),
            P("seq", None),
            P("seq", None),
            P("head", "seq"),
            P("head", "seq"),
        ),
        check_vma=False,
    )
```

profile of v0, /device:TPU:1, one launch (start us, length us, event | category | flops | bytes accessed | tf_op | source)
XLA Modules:
  0.0 992.9 jit_solution(1498079987410651189)
XLA Ops:
  13.9 2.6 rev.46
  23.7 23.2 %all-gather.1 = f32[8,4,1024]{2,1,0:T(4,128)S(1)} all-gather(f32[1,4,1024]{2,1,0:T(4,128)S(1)} %bitcast.653), channel_id=1, replica_groups=mesh['seq'=32,'head'=8] {'head'}, dimensions={0}, use_global_device_ids=true | all-gather | bytes 147456 | tf_op jit(solution)/shard_map/all_gather | solution.py:101
  48.7 21.8 %all-gather = f32[8,4,1024]{2,1,0:T(4,128)S(1)} all-gather(f32[1,4,1024]{2,1,0:T(4,128)S(1)} %bitcast.656), channel_id=1, replica_groups=mesh['seq'=32,'head'=8] {'head'}, dimensions={0}, use_global_device_ids=true | all-gather | bytes 147456 | tf_op jit(solution)/shard_map/all_gather | solution.py:102
  75.9 3.2 rev.45
  79.1 3.3 rev.47
  89.0 405.1 %while.92 = (s32[]{:T(128)}, f32[2,4,64,128]{3,2,1,0:T(8,128)S(1)}, f32[2,4,64,128]{3,2,1,0:T(8,128)S(1)}, f32[2,4]{1,0:T(2,128)S(1)}, f32[2,4,64,128]{3,2,1,0:T...) while((s32[]{:T(128)}, f32[2,4,64,128]{3,2,1,0:T(8,128)S(1)}, ...), condition=%wide.region_9.10_spmd, body=%wide.region_8.9_spmd.sunk | while | flops 262146 | bytes 3670245 | solution.py:136
  89.1 16.8 %collective-permute-start = (f32[2,4,64,128]{3,2,1,0:T(8,128)S(1)}, f32[2,4,64,128]{3,2,1,0:T(8,128)S(1)}, u32[]{:S(2)}, u32[]{:S(2)}) collective-permute-start(f32[2,4,64,128]{3,2,1,0:T(8,128)S(1)} %multiply_add_fusion.4), channel_id=1, source_target_pairs={{0,8},{8,16},{16,24},{24,32},{32,40},{40,48},{48,56},{56,64},{64,7... | collective-permute-start | bytes 786440 | tf_op jit(solution)/shard_map/while/body/eval_jaxpr/ppermute | solution.py:15
  109.2 4.5 collective-permute-done.1
  115.8 2.4 collective-permute-start.1
  119.0 4.8 collective-permute-done.1
  125.9 2.4 collective-permute-start.1
  129.1 4.8 collective-permute-done.1
  136.0 2.4 collective-permute-start.1
  139.2 7.2 collective-permute-done.1
  151.7 5.7 collective-permute-done.1
  162.7 5.7 collective-permute-done.1
  173.7 5.7 collective-permute-done.1
  184.8 5.7 collective-permute-done.1
  195.8 5.7 collective-permute-done.1
  206.8 5.7 collective-permute-done.1
  217.8 7.1 collective-permute-done.1
  230.3 7.5 collective-permute-done.1
  243.1 9.3 collective-permute-done.1
  257.7 6.9 collective-permute-done.1
  270.0 9.3 collective-permute-done.1
  284.6 6.9 collective-permute-done.1
  296.8 9.3 collective-permute-done.1
  311.4 6.9 collective-permute-done.1
  323.7 9.3 collective-permute-done.1
  338.3 6.9 collective-permute-done.1
  350.5 9.3 collective-permute-done.1
  365.1 6.9 collective-permute-done.1
  377.4 9.3 collective-permute-done.1
  392.0 6.9 collective-permute-done.1
  404.2 9.3 collective-permute-done.1
  418.8 6.9 collective-permute-done.1
  431.1 9.3 collective-permute-done.1
  445.7 6.9 collective-permute-done.1
  457.9 9.3 collective-permute-done.1
  472.5 6.9 collective-permute-done.1
  484.8 9.3 collective-permute-done.1
  496.3 30.3 %while.93 = (s32[]{:T(128)}, f32[4,64,128]{2,1,0:T(8,128)S(1)}, s32[]{:T(128)}, f32[4,4,64,128]{3,2,1,0:T(8,128)}, s32[4]{0:T(128)S(1)}, /*index=5*/f32[4,4,256]...) while((s32[]{:T(128)}, f32[4,64,128]{2,1,0:T(8,128)S(1)}, ...), condition=%wide.region_13.14_spmd, body=%wide.region_10.13_spmd.sunk | while | flops 100929552 | bytes 981141 | solution.py:57
  530.6 148.2 %while.94 = (s32[]{:T(128)}, f32[4,64,128]{2,1,0:T(8,128)S(1)}, f32[4,256,4,64]{1,0,3,2:T(4,128)}, f32[4,256,128]{2,1,0:T(8,128)}, f32[4,256,128]{2,1,0:T(8,128)...) while((s32[]{:T(128)}, f32[4,64,128]{2,1,0:T(8,128)S(1)}, ...), condition=%wide.region_27.28_spmd, body=%wide.region_14.27_spmd.sunk | while | flops 1214399488 | bytes 14093513 | solution.py:57
  550.0 6.7 dynamic_update_slice.137
  561.0 5.0 reduce-window.148
  587.1 6.7 dynamic_update_slice.137
  598.1 5.0 reduce-window.148
  624.1 6.7 dynamic_update_slice.137
  635.1 5.0 reduce-window.148
  661.2 6.7 dynamic_update_slice.137
  672.2 5.0 reduce-window.148
  680.2 36.9 %while.95 = (s32[]{:T(128)}, f32[4,64,128]{2,1,0:T(8,128)S(1)}, s32[]{:T(128)}, f32[4,4,64,128]{3,2,1,0:T(8,128)S(1)}, s32[4]{0:T(128)S(1)}, /*index=5*/f32[4,4,...) while((s32[]{:T(128)}, f32[4,64,128]{2,1,0:T(8,128)S(1)}, ...), condition=%wide.region_31.32_spmd, body=%wide.region_28.31_spmd.sunk | while | flops 100929552 | bytes 981141 | solution.py:57
  721.1 149.0 %while.96 = (s32[]{:T(128)}, f32[4,64,128]{2,1,0:T(8,128)S(1)}, f32[4,256,4,64]{1,0,3,2:T(4,128)}, f32[4,256,128]{2,1,0:T(8,128)}, f32[4,256,128]{2,1,0:T(8,128)...) while((s32[]{:T(128)}, f32[4,64,128]{2,1,0:T(8,128)S(1)}, ...), condition=%wide.region_45.46_spmd, body=%wide.region_32.45_spmd.sunk | while | flops 1214399488 | bytes 11734049 | solution.py:57
  740.8 6.7 dynamic_update_slice.144
  751.8 5.0 reduce-window.154
  778.1 6.7 dynamic_update_slice.144
  789.1 5.0 reduce-window.154
  815.3 6.7 dynamic_update_slice.144
  826.3 5.0 reduce-window.154
  852.6 6.7 dynamic_update_slice.144
  863.6 5.0 reduce-window.154
  870.2 3.5 rev.51
  885.5 2.5 copy.260
  889.3 91.3 %all-reduce.9.cloned.1.call-done = (f32[1024,128]{1,0:T(8,128)}, f32[1024,128]{1,0:T(8,128)}, f32[32,1024]{1,0:T(8,128)}, f32[32,1024]{1,0:T(8,128)}) async-done(((f32[1024,128]{1,0:T(8,128)}, f32[1024,128]{1,0:T(8,128)}, f32[32,1024]{1,0:T(8,128)}, f32[32,1024]{1,0:T(8,128)}), (f32[1024,128]{1,0:T(8,128)}, f32[1024,128]{1,0:T(8,128)}, f32[32,1024]{1,0:T(8,128)}, ...) | async-done | bytes 1310736 | tf_op jit(solution)/shard_map/psum | solution.py:168
  (1174 shorter events, 473.6 us)
Async XLA Ops:
  7.2 973.4 %all-reduce.9.cloned.1.call-start = ((), (), s32[]{:S(2)}) async-start(), calls=%async_computation | async-start | bytes 2621440 | tf_op jit(solution)/shard_map/psum | solution.py:168
  89.1 20.1 %collective-permute-start = (f32[2,4,64,128]{3,2,1,0:T(8,128)S(1)}, f32[2,4,64,128]{3,2,1,0:T(8,128)S(1)}, u32[]{:S(2)}, u32[]{:S(2)}) collective-permute-start(f32[2,4,64,128]{3,2,1,0:T(8,128)S(1)} %multiply_add_fusion.4), channel_id=1, source_target_pairs={{0,8},{8,16},{16,24},{24,32},{32,40},{40,48},{48,56},{56,64},{64,7... | collective-permute-start | bytes 786440 | tf_op jit(solution)/shard_map/while/body/eval_jaxpr/ppermute | solution.py:15
  106.0 7.7 collective-permute-start.1
  113.8 5.2 collective-permute-start
  115.8 8.0 collective-permute-start.1
  123.9 5.2 collective-permute-start
  125.9 8.0 collective-permute-start.1
  134.0 5.2 collective-permute-start
  136.0 10.4 %collective-permute-start.1 = (f32[2,4,64,128]{3,2,1,0:T(8,128)S(1)}, f32[2,4,64,128]{3,2,1,0:T(8,128)S(1)}, u32[]{:S(2)}, u32[]{:S(2)}) collective-permute-start(f32[2,4,64,128]{3,2,1,0:T(8,128)S(1)} %multiply_add_fusion.5), channel_id=1, source_target_pairs={{8,0},{16,8},{24,16},{32,24},{40,32},{48,40},{56,48},{64,56},{72,6... | collective-permute-start | bytes 786440 | tf_op jit(solution)/shard_map/while/body/eval_jaxpr/ppermute | solution.py:15
  146.5 5.2 collective-permute-start
  148.5 8.9 collective-permute-start.1
  157.5 5.2 collective-permute-start
  159.5 8.9 collective-permute-start.1
  168.5 5.2 collective-permute-start
  170.5 8.9 collective-permute-start.1
  179.5 5.2 collective-permute-start
  181.6 8.9 collective-permute-start.1
  190.6 5.2 collective-permute-start
  192.6 8.9 collective-permute-start.1
  201.6 5.2 collective-permute-start
  203.6 8.9 collective-permute-start.1
  212.6 5.2 collective-permute-start
  214.6 10.3 %collective-permute-start.1 = (f32[2,4,64,128]{3,2,1,0:T(8,128)S(1)}, f32[2,4,64,128]{3,2,1,0:T(8,128)S(1)}, u32[]{:S(2)}, u32[]{:S(2)}) collective-permute-start(f32[2,4,64,128]{3,2,1,0:T(8,128)S(1)} %multiply_add_fusion.5), channel_id=1, source_target_pairs={{8,0},{16,8},{24,16},{32,24},{40,32},{48,40},{56,48},{64,56},{72,6... | collective-permute-start | bytes 786440 | tf_op jit(solution)/shard_map/while/body/eval_jaxpr/ppermute | solution.py:15
  225.1 5.2 collective-permute-start
  227.1 10.7 %collective-permute-start.1 = (f32[2,4,64,128]{3,2,1,0:T(8,128)S(1)}, f32[2,4,64,128]{3,2,1,0:T(8,128)S(1)}, u32[]{:S(2)}, u32[]{:S(2)}) collective-permute-start(f32[2,4,64,128]{3,2,1,0:T(8,128)S(1)} %multiply_add_fusion.5), channel_id=1, source_target_pairs={{8,0},{16,8},{24,16},{32,24},{40,32},{48,40},{56,48},{64,56},{72,6... | collective-permute-start | bytes 786440 | tf_op jit(solution)/shard_map/while/body/eval_jaxpr/ppermute | solution.py:15
  237.9 5.2 collective-permute-start
  239.9 12.5 %collective-permute-start.1 = (f32[2,4,64,128]{3,2,1,0:T(8,128)S(1)}, f32[2,4,64,128]{3,2,1,0:T(8,128)S(1)}, u32[]{:S(2)}, u32[]{:S(2)}) collective-permute-start(f32[2,4,64,128]{3,2,1,0:T(8,128)S(1)} %multiply_add_fusion.5), channel_id=1, source_target_pairs={{8,0},{16,8},{24,16},{32,24},{40,32},{48,40},{56,48},{64,56},{72,6... | collective-permute-start | bytes 786440 | tf_op jit(solution)/shard_map/while/body/eval_jaxpr/ppermute | solution.py:15
  252.5 5.2 collective-permute-start
  254.5 10.1 %collective-permute-start.1 = (f32[2,4,64,128]{3,2,1,0:T(8,128)S(1)}, f32[2,4,64,128]{3,2,1,0:T(8,128)S(1)}, u32[]{:S(2)}, u32[]{:S(2)}) collective-permute-start(f32[2,4,64,128]{3,2,1,0:T(8,128)S(1)} %multiply_add_fusion.5), channel_id=1, source_target_pairs={{8,0},{16,8},{24,16},{32,24},{40,32},{48,40},{56,48},{64,56},{72,6... | collective-permute-start | bytes 786440 | tf_op jit(solution)/shard_map/while/body/eval_jaxpr/ppermute | solution.py:15
  264.8 5.2 collective-permute-start
  266.8 12.5 %collective-permute-start.1 = (f32[2,4,64,128]{3,2,1,0:T(8,128)S(1)}, f32[2,4,64,128]{3,2,1,0:T(8,128)S(1)}, u32[]{:S(2)}, u32[]{:S(2)}) collective-permute-start(f32[2,4,64,128]{3,2,1,0:T(8,128)S(1)} %multiply_add_fusion.5), channel_id=1, source_target_pairs={{8,0},{16,8},{24,16},{32,24},{40,32},{48,40},{56,48},{64,56},{72,6... | collective-permute-start | bytes 786440 | tf_op jit(solution)/shard_map/while/body/eval_jaxpr/ppermute | solution.py:15
  279.4 5.2 collective-permute-start
  281.4 10.1 %collective-permute-start.1 = (f32[2,4,64,128]{3,2,1,0:T(8,128)S(1)}, f32[2,4,64,128]{3,2,1,0:T(8,128)S(1)}, u32[]{:S(2)}, u32[]{:S(2)}) collective-permute-start(f32[2,4,64,128]{3,2,1,0:T(8,128)S(1)} %multiply_add_fusion.5), channel_id=1, source_target_pairs={{8,0},{16,8},{24,16},{32,24},{40,32},{48,40},{56,48},{64,56},{72,6... | collective-permute-start | bytes 786440 | tf_op jit(solution)/shard_map/while/body/eval_jaxpr/ppermute | solution.py:15
  291.6 5.2 collective-permute-start
  293.6 12.5 %collective-permute-start.1 = (f32[2,4,64,128]{3,2,1,0:T(8,128)S(1)}, f32[2,4,64,128]{3,2,1,0:T(8,128)S(1)}, u32[]{:S(2)}, u32[]{:S(2)}) collective-permute-start(f32[2,4,64,128]{3,2,1,0:T(8,128)S(1)} %multiply_add_fusion.5), channel_id=1, source_target_pairs={{8,0},{16,8},{24,16},{32,24},{40,32},{48,40},{56,48},{64,56},{72,6... | collective-permute-start | bytes 786440 | tf_op jit(solution)/shard_map/while/body/eval_jaxpr/ppermute | solution.py:15
  306.2 5.2 collective-permute-start
  308.2 10.1 %collective-permute-start.1 = (f32[2,4,64,128]{3,2,1,0:T(8,128)S(1)}, f32[2,4,64,128]{3,2,1,0:T(8,128)S(1)}, u32[]{:S(2)}, u32[]{:S(2)}) collective-permute-start(f32[2,4,64,128]{3,2,1,0:T(8,128)S(1)} %multiply_add_fusion.5), channel_id=1, source_target_pairs={{8,0},{16,8},{24,16},{32,24},{40,32},{48,40},{56,48},{64,56},{72,6... | collective-permute-start | bytes 786440 | tf_op jit(solution)/shard_map/while/body/eval_jaxpr/ppermute | solution.py:15
  318.5 5.2 collective-permute-start
  320.5 12.5 %collective-permute-start.1 = (f32[2,4,64,128]{3,2,1,0:T(8,128)S(1)}, f32[2,4,64,128]{3,2,1,0:T(8,128)S(1)}, u32[]{:S(2)}, u32[]{:S(2)}) collective-permute-start(f32[2,4,64,128]{3,2,1,0:T(8,128)S(1)} %multiply_add_fusion.5), channel_id=1, source_target_pairs={{8,0},{16,8},{24,16},{32,24},{40,32},{48,40},{56,48},{64,56},{72,6... | collective-permute-start | bytes 786440 | tf_op jit(solution)/shard_map/while/body/eval_jaxpr/ppermute | solution.py:15
  333.1 5.2 collective-permute-start
  335.1 10.1 %collective-permute-start.1 = (f32[2,4,64,128]{3,2,1,0:T(8,128)S(1)}, f32[2,4,64,128]{3,2,1,0:T(8,128)S(1)}, u32[]{:S(2)}, u32[]{:S(2)}) collective-permute-start(f32[2,4,64,128]{3,2,1,0:T(8,128)S(1)} %multiply_add_fusion.5), channel_id=1, source_target_pairs={{8,0},{16,8},{24,16},{32,24},{40,32},{48,40},{56,48},{64,56},{72,6... | collective-permute-start | bytes 786440 | tf_op jit(solution)/shard_map/while/body/eval_jaxpr/ppermute | solution.py:15
  345.3 5.2 collective-permute-start
  347.3 12.5 %collective-permute-start.1 = (f32[2,4,64,128]{3,2,1,0:T(8,128)S(1)}, f32[2,4,64,128]{3,2,1,0:T(8,128)S(1)}, u32[]{:S(2)}, u32[]{:S(2)}) collective-permute-start(f32[2,4,64,128]{3,2,1,0:T(8,128)S(1)} %multiply_add_fusion.5), channel_id=1, source_target_pairs={{8,0},{16,8},{24,16},{32,24},{40,32},{48,40},{56,48},{64,56},{72,6... | collective-permute-start | bytes 786440 | tf_op jit(solution)/shard_map/while/body/eval_jaxpr/ppermute | solution.py:15
  359.9 5.2 collective-permute-start
  361.9 10.1 %collective-permute-start.1 = (f32[2,4,64,128]{3,2,1,0:T(8,128)S(1)}, f32[2,4,64,128]{3,2,1,0:T(8,128)S(1)}, u32[]{:S(2)}, u32[]{:S(2)}) collective-permute-start(f32[2,4,64,128]{3,2,1,0:T(8,128)S(1)} %multiply_add_fusion.5), channel_id=1, source_target_pairs={{8,0},{16,8},{24,16},{32,24},{40,32},{48,40},{56,48},{64,56},{72,6... | collective-permute-start | bytes 786440 | tf_op jit(solution)/shard_map/while/body/eval_jaxpr/ppermute | solution.py:15
  372.2 5.2 collective-permute-start
  374.2 12.5 %collective-permute-start.1 = (f32[2,4,64,128]{3,2,1,0:T(8,128)S(1)}, f32[2,4,64,128]{3,2,1,0:T(8,128)S(1)}, u32[]{:S(2)}, u32[]{:S(2)}) collective-permute-start(f32[2,4,64,128]{3,2,1,0:T(8,128)S(1)} %multiply_add_fusion.5), channel_id=1, source_target_pairs={{8,0},{16,8},{24,16},{32,24},{40,32},{48,40},{56,48},{64,56},{72,6... | collective-permute-start | bytes 786440 | tf_op jit(solution)/shard_map/while/body/eval_jaxpr/ppermute | solution.py:15
  386.8 5.2 collective-permute-start
  388.8 10.1 %collective-permute-start.1 = (f32[2,4,64,128]{3,2,1,0:T(8,128)S(1)}, f32[2,4,64,128]{3,2,1,0:T(8,128)S(1)}, u32[]{:S(2)}, u32[]{:S(2)}) collective-permute-start(f32[2,4,64,128]{3,2,1,0:T(8,128)S(1)} %multiply_add_fusion.5), channel_id=1, source_target_pairs={{8,0},{16,8},{24,16},{32,24},{40,32},{48,40},{56,48},{64,56},{72,6... | collective-permute-start | bytes 786440 | tf_op jit(solution)/shard_map/while/body/eval_jaxpr/ppermute | solution.py:15
  399.0 5.2 collective-permute-start
  401.0 12.5 %collective-permute-start.1 = (f32[2,4,64,128]{3,2,1,0:T(8,128)S(1)}, f32[2,4,64,128]{3,2,1,0:T(8,128)S(1)}, u32[]{:S(2)}, u32[]{:S(2)}) collective-permute-start(f32[2,4,64,128]{3,2,1,0:T(8,128)S(1)} %multiply_add_fusion.5), channel_id=1, source_target_pairs={{8,0},{16,8},{24,16},{32,24},{40,32},{48,40},{56,48},{64,56},{72,6... | collective-permute-start | bytes 786440 | tf_op jit(solution)/shard_map/while/body/eval_jaxpr/ppermute | solution.py:15
  413.6 5.2 collective-permute-start
  415.6 10.1 %collective-permute-start.1 = (f32[2,4,64,128]{3,2,1,0:T(8,128)S(1)}, f32[2,4,64,128]{3,2,1,0:T(8,128)S(1)}, u32[]{:S(2)}, u32[]{:S(2)}) collective-permute-start(f32[2,4,64,128]{3,2,1,0:T(8,128)S(1)} %multiply_add_fusion.5), channel_id=1, source_target_pairs={{8,0},{16,8},{24,16},{32,24},{40,32},{48,40},{56,48},{64,56},{72,6... | collective-permute-start | bytes 786440 | tf_op jit(solution)/shard_map/while/body/eval_jaxpr/ppermute | solution.py:15
  425.9 5.2 collective-permute-start
  427.9 12.5 %collective-permute-start.1 = (f32[2,4,64,128]{3,2,1,0:T(8,128)S(1)}, f32[2,4,64,128]{3,2,1,0:T(8,128)S(1)}, u32[]{:S(2)}, u32[]{:S(2)}) collective-permute-start(f32[2,4,64,128]{3,2,1,0:T(8,128)S(1)} %multiply_add_fusion.5), channel_id=1, source_target_pairs={{8,0},{16,8},{24,16},{32,24},{40,32},{48,40},{56,48},{64,56},{72,6... | collective-permute-start | bytes 786440 | tf_op jit(solution)/shard_map/while/body/eval_jaxpr/ppermute | solution.py:15
  440.5 5.2 collective-permute-start
  442.5 10.1 %collective-permute-start.1 = (f32[2,4,64,128]{3,2,1,0:T(8,128)S(1)}, f32[2,4,64,128]{3,2,1,0:T(8,128)S(1)}, u32[]{:S(2)}, u32[]{:S(2)}) collective-permute-start(f32[2,4,64,128]{3,2,1,0:T(8,128)S(1)} %multiply_add_fusion.5), channel_id=1, source_target_pairs={{8,0},{16,8},{24,16},{32,24},{40,32},{48,40},{56,48},{64,56},{72,6... | collective-permute-start | bytes 786440 | tf_op jit(solution)/shard_map/while/body/eval_jaxpr/ppermute | solution.py:15
  452.7 5.2 collective-permute-start
  454.7 12.5 %collective-permute-start.1 = (f32[2,4,64,128]{3,2,1,0:T(8,128)S(1)}, f32[2,4,64,128]{3,2,1,0:T(8,128)S(1)}, u32[]{:S(2)}, u32[]{:S(2)}) collective-permute-start(f32[2,4,64,128]{3,2,1,0:T(8,128)S(1)} %multiply_add_fusion.5), channel_id=1, source_target_pairs={{8,0},{16,8},{24,16},{32,24},{40,32},{48,40},{56,48},{64,56},{72,6... | collective-permute-start | bytes 786440 | tf_op jit(solution)/shard_map/while/body/eval_jaxpr/ppermute | solution.py:15
  467.3 5.2 collective-permute-start
  469.3 10.1 %collective-permute-start.1 = (f32[2,4,64,128]{3,2,1,0:T(8,128)S(1)}, f32[2,4,64,128]{3,2,1,0:T(8,128)S(1)}, u32[]{:S(2)}, u32[]{:S(2)}) collective-permute-start(f32[2,4,64,128]{3,2,1,0:T(8,128)S(1)} %multiply_add_fusion.5), channel_id=1, source_target_pairs={{8,0},{16,8},{24,16},{32,24},{40,32},{48,40},{56,48},{64,56},{72,6... | collective-permute-start | bytes 786440 | tf_op jit(solution)/shard_map/while/body/eval_jaxpr/ppermute | solution.py:15
  479.6 5.2 collective-permute-start
  481.6 12.5 %collective-permute-start.1 = (f32[2,4,64,128]{3,2,1,0:T(8,128)S(1)}, f32[2,4,64,128]{3,2,1,0:T(8,128)S(1)}, u32[]{:S(2)}, u32[]{:S(2)}) collective-permute-start(f32[2,4,64,128]{3,2,1,0:T(8,128)S(1)} %multiply_add_fusion.5), channel_id=1, source_target_pairs={{8,0},{16,8},{24,16},{32,24},{40,32},{48,40},{56,48},{64,56},{72,6... | collective-permute-start | bytes 786440 | tf_op jit(solution)/shard_map/while/body/eval_jaxpr/ppermute | solution.py:15
  888.0 92.6 %copy-start.56 = (f32[4,4,256]{2,1,0:T(4,128)S(1)}, f32[4,4,256]{2,1,0:T(4,128)}, u32[]{:S(2)}) copy-start(f32[4,4,256]{2,1,0:T(4,128)} %get-tuple-element.813) | copy-start | bytes 49156
  (210 other events, 340.2 us)
Sparse Core Ops, SparseCore 0:
  880.0 100.5 all-reduce.8
where the time goes:
time: 1000 us; the launch traced here: 993 us
  waiting for transfers between devices  341 us (34%)
  local copies, waits for them, and re-layouts  213 us (21%)
  starting transfers between devices  149 us (15%)
  other arithmetic  139 us (14%)
  matrix products  81.8 us (8%)
  blocking collectives  45 us (4%)
  between operations  16.4 us (2%)
    ppermute x62, waiting for transfers between devices, shifted(): lax.ppermute(value, axis, [(source, source + steps) for source in range(l...  250 us
    ppermute x62, starting transfers between devices, shifted(): lax.ppermute(value, axis, [(source, source + steps) for source in range(l...  149 us
    psum x1, waiting for transfers between devices, on_device(): write_grad, read_grad = lax.psum((gradients[1], gradients[2]), 'head')  91.3 us
    dynamic_update_slice x40, local copies, waits for them, and re-layouts, strand(): lax.scan(jax.checkpoint(block_step), (state_in, seg_before), blocks)  64.5 us
    another operation x60, other arithmetic  63.8 us
    dot_general x16, matrix products, block_step(): inside = jnp.einsum('hts,shp->thp', weights, values, precision=highest)  27.7 us
    while x384, local copies, waits for them, and re-layouts  26.7 us
    dynamic_slice x32, local copies, waits for them, and re-layouts, strand(): lax.scan(jax.checkpoint(block_step), (state_in, seg_before), blocks)  25.5 us
  transfers between devices with their start and end apart: 63, of which 63 were waited for; matrix products, arithmetic and copies ran while one was open for 1% of the time, Pallas kernels for 0%

commit v1 on v0

v1 whole, which is shorter than its diff:
```python
import functools

import jax
import jax.numpy as jnp
from jax import lax
from jax.experimental import pallas as pl
from jax.experimental.pallas import tpu as pltpu
from jax.sharding import PartitionSpec as P

Q = 256
STRIP = 32
LOG2E = 1.4426950408889634
F32, BF16 = jnp.float32, jnp.bfloat16
MESH = pl.DeviceIdType.MESH
VMEM_LIMIT = 56 * 1024 * 1024


def iota(shape, dim):
    return lax.broadcasted_iota(jnp.int32, shape, dim)


def split2(v):
    hi = v.astype(BF16)
    return hi, (v - hi.astype(F32)).astype(BF16)


def split3(v):
    hi = v.astype(BF16)
    rest = v - hi.astype(F32)
    mid = rest.astype(BF16)
    return hi, mid, (rest - mid.astype(F32)).astype(BF16)


def dot(a, b):
    return lax.dot_general(a, b, (((1,), (0,)), ((), ())), preferred_element_type=F32)


def dot_nt(a, b):
    return lax.dot_general(a, b, (((1,), (1,)), ((), ())), preferred_element_type=F32)


def dot_sum(parts, b, how=dot):
    total = how(parts[0], b)
    for part in parts[1:]:
        total = total + how(part, b)
    return total


def segment_at(starts_ref, t):
    total = (starts_ref[0] <= t).astype(jnp.int32)
    for k in range(1, 4):
        total = total + (starts_ref[k] <= t).astype(jnp.int32)
    return total


FRONT, MIRROR = slice(0, 256), slice(256, 512)
STRANDS = (FRONT, MIRROR)


def kernel(
    nh,
    ns,
    heads_ref,
    starts_ref,
    x_ref,
    g_ref,
    b_ref,
    c_ref,
    step_ref,
    decay_ref,
    dx_ref,
    sums_ref,
    dstep_ref,
    ddecay_ref,
    all_ref,
    rows_ref,
    cols_ref,
    xhi_ref,
    xlo_ref,
    ghi_ref,
    glo_ref,
    el_ref,
    ends_ref,
    seeds_ref,
    gain_ref,
    pair_out,
    pair_in,
    slice_out,
    slice_in,
    scan_out,
    total_out,
    total_in,
    back_in,
    next_out,
    entering,
    states,
    adjoints,
    gm,
    pt,
    whi,
    wlo,
    dghi,
    dglo,
    csum,
    row_keep,
    col_keep,
    part,
    got,
    own_ref,
    other_ref,
    others,
    gather_sems,
    pair_sems,
    z_sems,
    head_sems,
    other_sems,
):
    length = x_ref.shape[0]
    chunks = length // Q
    head_me = lax.axis_index("head")
    seq_me = lax.axis_index("seq")
    offset = seq_me * length
    core = lax.rem(seq_me, 2)
    zs = ns // 4
    z_me = lax.rem(seq_me // 2, zs)
    x_me = seq_me // (2 * zs)
    core_peer = seq_me + 1 - 2 * core
    x_peer = lax.rem(seq_me + ns // 2, ns)

    def z_peer(k):
        z = lax.rem(z_me + k, zs)
        return z, x_me * 2 * zs + z * 2 + core

    all_ref[head_me, 0:4, :] = step_ref[...]
    all_ref[head_me, 4:8, :] = decay_ref[...]
    barrier = pltpu.get_barrier_semaphore()

    def greet_head(k, carry):
        peer = lax.rem(head_me + k, nh)
        pl.semaphore_signal(barrier, inc=1, device_id={"head": peer}, device_id_type=MESH)
        return carry

    def greet_z(k, carry):
        pl.semaphore_signal(barrier, inc=1, device_id={"seq": z_peer(k)[1]}, device_id_type=MESH)
        return carry

    lax.fori_loop(1, nh, greet_head, 0)
    lax.fori_loop(1, zs, greet_z, 0)
    pl.semaphore_signal(barrier, inc=1, device_id={"seq": core_peer}, device_id_type=MESH)
    pl.semaphore_signal(barrier, inc=1, device_id={"seq": x_peer}, device_id_type=MESH)
    pl.semaphore_wait(barrier, nh + zs)

    def remote(source, target, send, recv, axis, peer):
        return pltpu.make_async_remote_copy(
            src_ref=source,
            dst_ref=target,
            send_sem=send,
            recv_sem=recv,
            device_id={axis: peer},
            device_id_type=MESH,
        )

    def every(count, copy):
        def begin(k, carry):
            copy(k).start()
            return carry

        def end(k, carry):
            copy(k).wait()
            return carry

        lax.fori_loop(1, count, begin, 0)
        return lambda: lax.fori_loop(1, count, end, 0)

    def head_copies(source, target, send, recv):
        def copy(k):
            peer = lax.rem(head_me + k, nh)
            return remote(source(peer), target, send.at[k], recv.at[k], "head", peer)

        return every(nh, copy)

    def z_copies(source, target, send, recv):
        def copy(k):
            z, peer = z_peer(k)
            return remote(source(z), target, send.at[k], recv.at[k], "seq", peer)

        return every(zs, copy)

    gathered = head_copies(
        lambda peer: all_ref.at[head_me], all_ref.at[head_me], gather_sems.at[0], gather_sems.at[1]
    )

    lower = iota((Q, Q), 0) >= iota((Q, Q), 1)
    upper = iota((Q, Q), 0) <= iota((Q, Q), 1)
    low_one = jnp.where(lower, 1.0, 0.0).astype(BF16)
    up_one = jnp.where(upper, 1.0, 0.0).astype(BF16)
    lane = iota((16, 512), 1)
    source = jnp.where(lane < 256, 8, 4) + (lane % 256) // 64
    spread = jnp.where(iota((16, 512), 0) == source, 1.0, 0.0).astype(BF16)
    pick8 = jnp.where(iota((8, 256), 0) == iota((8, 256), 1) // 64, 1.0, 0.0)


    def prepare(strand):
        def chunk(c, carry):
            base = pl.multiple_of(c * Q, Q)
            span = pl.ds(base, Q)
            if strand == 0:
                s4 = all_ref[head_me, 0:4, span]
                d4 = all_ref[head_me, 4:8, span]
            else:
                heads = [heads_ref[head_me * 4 + h] for h in range(4)]
                s4 = jnp.concatenate([all_ref[i // 4, pl.ds(i % 4, 1), span] for i in heads], axis=0)
                d4 = jnp.concatenate([all_ref[i // 4, pl.ds(i % 4 + 4, 1), span] for i in heads], axis=0)
            s8 = jnp.concatenate([s4, s4], axis=0)
            d8 = jnp.concatenate([d4, d4], axis=0)
            cum8 = dot_sum(split3(d8), low_one if strand else up_one) * LOG2E
            total8 = cum8[:, 0:1] if strand else cum8[:, Q - 1 : Q]
            first = offset + base
            seg = segment_at(starts_ref, first + iota((8, Q), 1))
            seg_first, seg_last = segment_at(starts_ref, first), segment_at(starts_ref, first + Q - 1)
            if strand:
                seg_in, seg_near, seg_far = segment_at(starts_ref, first + Q), seg_last, seg_first
            else:
                seg_in = jnp.where(first == 0, -1, segment_at(starts_ref, first - 1))
                seg_near, seg_far = seg_first, seg_last
            del seg_near
            e8 = jnp.where(seg == seg_in, jnp.exp2(cum8), 0.0)
            l8 = jnp.where(seg == seg_far, jnp.exp2(total8 - cum8) * s8, 0.0)
            gain8 = jnp.exp2(total8) * (seg_in == seg_far).astype(F32)
            gain = jnp.sum(pick8 * gain8, axis=0, keepdims=True)
            gain_ref[c, :, STRANDS[strand]] = jnp.broadcast_to(gain, (8, 256))
            rows = jnp.concatenate([cum8[0:4], e8[0:4], l8[0:4], s8[0:4]], axis=0)
            rows_ref[c, strand] = rows
            cols = rows.T
            cols_ref[strand, span, :] = cols
            wide = dot_sum(split3(cols), spread)
            lanes = STRANDS[strand]
            el_ref[span, lanes] = wide[:, 0:256]
            xhi, xlo = split2(x_ref[span, :].astype(F32) * wide[:, 0:256])
            ghi, glo = split2(g_ref[span, :].astype(F32) * wide[:, 256:512])
            xhi_ref[span, lanes] = xhi
            xlo_ref[span, lanes] = xlo
            ghi_ref[span, lanes] = ghi
            glo_ref[span, lanes] = glo
            bt, ct = b_ref[span, :].T, c_ref[span, :].T
            ends_ref[c, :, lanes] = dot(bt, xhi) + dot(bt, xlo)
            seeds_ref[c, :, lanes] = dot(ct, ghi) + dot(ct, glo)
            return carry

        lax.fori_loop(0, chunks, chunk, 0)

    prepare(0)
    gathered()
    prepare(1)

    whole = gain_ref[0]
    for c in range(1, chunks):
        whole = whole * gain_ref[c]
    ascending, descending = range(chunks), range(chunks - 1, -1, -1)
    quantities = (
        (ends_ref, FRONT, ascending),
        (seeds_ref, MIRROR, ascending),
        (ends_ref, MIRROR, descending),
        (seeds_ref, FRONT, descending),
    )
    for q, (terms, lanes, order) in enumerate(quantities):
        run = None
        for c in order:
            run = terms[c, :, lanes] if run is None else run * gain_ref[c, 0:1, lanes] + terms[c, :, lanes]
        for k in range(2):
            pair_out[q // 2, (q % 2) * 256 + k * 128 : (q % 2) * 256 + (k + 1) * 128] = run[:, k * 128 : (k + 1) * 128]
    for p in range(2):
        for a in range(2):
            lanes = STRANDS[(p + a) % 2]
            gains = whole[:, lanes]
            for k in range(2):
                pair_out[p, 512 + (a * 2 + k) * 8 : 512 + (a * 2 + k + 1) * 8] = gains[:, k * 128 : (k + 1) * 128]


    half_mask = [jnp.where(iota((1, 128), 1) // 64 == k, 1.0, 0.0).astype(BF16) for k in range(2)]
    zero_row = jnp.zeros((8, 128), F32)
    part_rows = Q // nh

    def put_part(c, lanes, value):
        part[c, :, :, lanes] = value.reshape(nh, part_rows, 128)

    def inside(c):
        base = c * Q
        span = slice(base, base + Q)
        first = offset + base
        bc, cc = b_ref[span, :], c_ref[span, :]
        xs = [x_ref[span, k * 128 : (k + 1) * 128] for k in range(2)]
        gs = [g_ref[span, k * 128 : (k + 1) * 128] for k in range(2)]
        seg_s = segment_at(starts_ref, first + iota((Q, 1), 0))
        seg_t = segment_at(starts_ref, first + iota((1, Q), 1))
        gm[...] = jnp.where(seg_s == seg_t, dot_nt(bc, cc), 0.0)
        for h in range(4):
            pt[h] = dot_nt(xs[h // 2] * half_mask[h % 2], gs[h // 2])
        row_sums = []
        for i in range(2):

            def strip(r, sums, i=i):
                start = pl.multiple_of(i * 128 + r * STRIP, STRIP)
                at = pl.ds(start, STRIP)
                at_cols = pl.ds(pl.multiple_of(base + start, STRIP), STRIP)
                col_f, col_m = cols_ref[0, at_cols, :], cols_ref[1, at_cols, :]
                lane128 = iota((STRIP, 128), 1)
                s_index = r * STRIP + iota((STRIP, 128), 0)
                ahead = lane128 > s_index
                behind = lane128 < s_index
                sums = list(sums)
                collected = jnp.zeros((STRIP, 128), F32)
                dg = [jnp.zeros((STRIP, 128), F32) for _ in range(2)]
                for h in range(4):
                    cum_f, cum_m = col_f[:, h : h + 1], col_m[:, h : h + 1]
                    step_f, step_m = col_f[:, 12 + h : 13 + h], col_m[:, 12 + h : 13 + h]
                    lane_sums = [None, None]
                    for j in range(2):
                        t = slice(j * 128, (j + 1) * 128)
                        row_f = rows_ref[c, 0, h : h + 1, t]
                        row_m = rows_ref[c, 1, h : h + 1, t]
                        if i == j:
                            gap = jnp.where(behind, row_m - cum_m, row_f - cum_f)
                            step = jnp.where(behind, step_m, jnp.where(ahead, step_f, step_f + step_m))
                        elif j > i:
                            gap, step = row_f - cum_f, step_f
                        else:
                            gap, step = row_m - cum_m, step_m
                        d = jnp.exp2(gap) * step
                        w = d * gm[at, t]
                        p = pt[h, at, t]
                        dg[j] = dg[j] + d * p
                        e = w * p
                        hi, lo = split2(w)
                        whi[h, at, t] = hi
                        wlo[h, at, t] = lo
                        if i == j:
                            parts = [jnp.where(ahead, e, 0.0), jnp.where(behind, e, 0.0)]
                        else:
                            parts = [e, None] if j > i else [None, e]
                        for strand in range(2):
                            piece = parts[strand]
                            if piece is None:
                                continue
                            slot = (h * 2 + j) * 2 + strand
                            add = piece[0:8]
                            for u in range(1, STRIP // 8):
                                add = add + piece[u * 8 : (u + 1) * 8]
                            sums[slot] = sums[slot] + add
                            old = lane_sums[strand]
                            lane_sums[strand] = piece if old is None else old + piece
                    for strand in range(2):
                        total = jnp.sum(lane_sums[strand], axis=1, keepdims=True)
                        collected = jnp.where(lane128 == strand * 4 + h, total, collected)
                csum[at, :] = collected
                rows_at = segment_at(starts_ref, first + start + iota((STRIP, 1), 0))
                for j in range(2):
                    t = slice(j * 128, (j + 1) * 128)
                    cols_at = segment_at(starts_ref, first + j * 128 + iota((1, 128), 1))
                    hi, lo = split2(jnp.where(rows_at == cols_at, dg[j], 0.0))
                    dghi[at, t] = hi
                    dglo[at, t] = lo
                return tuple(sums)

            row_sums.append(lax.fori_loop(0, 128 // STRIP, strip, (zero_row,) * 16))
        rows_in = []
        for strand in range(2):
            for h in range(4):
                lanes = []
                for j in range(2):
                    slot = (h * 2 + j) * 2 + strand
                    lanes.append(jnp.sum(row_sums[0][slot] + row_sums[1][slot], axis=0, keepdims=True))
                rows_in.append(jnp.concatenate(lanes, axis=1))
        row_keep[c] = jnp.concatenate(rows_in, axis=0)
        col_keep[c] = csum[...].T[0:8]
        for k in range(2):
            total = None
            for h in (2 * k, 2 * k + 1):
                masked = gs[k] * half_mask[h % 2]
                term = dot(whi[h], masked) + dot(wlo[h], masked)
                total = term if total is None else total + term
            dx_ref[span, k * 128 : (k + 1) * 128] = total
        put_part(c, slice(0, 128), dot(dghi[...], cc) + dot(dglo[...], cc))
        dgt_hi, dgt_lo = dghi[...].T, dglo[...].T
        put_part(c, slice(128, 256), dot(dgt_hi, bc) + dot(dgt_lo, bc))


    other = 1 - core
    trade = remote(pair_out.at[other], pair_in, pair_sems.at[0], pair_sems.at[1], "seq", core_peer)
    trade.start()
    inside(0)
    trade.wait()

    def gain_of(ref, a, k):
        return ref[512 + (a * 2 + k) * 8 : 512 + (a * 2 + k + 1) * 8][0:1]

    mine = pair_out.at[core]
    slice_rows = 256 // zs
    for a in range(2):
        for k in range(2):
            rows = slice(a * 256 + k * 128, a * 256 + (k + 1) * 128)
            chip = gain_of(pair_in, a, k) * mine[rows] + pair_in[rows]
            slices = slice(k * (zs // 2), (k + 1) * (zs // 2))
            slice_out[slices, a * slice_rows : (a + 1) * slice_rows] = chip.reshape(zs // 2, slice_rows, 128)
    for k in range(2):
        gains = [gain_of(pair_in, a, k) * gain_of(mine, a, k) for a in range(2)]
        both = jnp.where(iota((8, 128), 0) < 4, gains[0], gains[1])
        slices = slice(k * (zs // 2), (k + 1) * (zs // 2))
        slice_out[slices, 2 * slice_rows : 2 * slice_rows + 8] = jnp.broadcast_to(both[None], (zs // 2, 8, 128))
    slice_in[z_me] = slice_out[z_me]
    sliced = z_copies(lambda z: slice_out.at[z], slice_in.at[z_me], z_sems.at[0], z_sems.at[1])
    inside(1)
    sliced()

    def order(i):
        return i + core * (zs - 1 - 2 * i)

    runs = [jnp.zeros((slice_rows, 128), F32) for _ in range(2)]
    for i in range(zs):
        z = order(i)
        for a in range(2):
            rows = slice(a * slice_rows, (a + 1) * slice_rows)
            scan_out[z, rows] = runs[a]
            gain = slice_in[z, 2 * slice_rows + a * 4 : 2 * slice_rows + a * 4 + 1]
            runs[a] = gain * runs[a] + slice_in[z, rows]
    for a in range(2):
        total_out[a * slice_rows : (a + 1) * slice_rows] = runs[a]
    swap = remote(total_out, total_in, pair_sems.at[2], pair_sems.at[3], "seq", x_peer)
    swap.start()
    inside(2)
    swap.wait()
    second = jnp.where(x_me == 1 - core, 1.0, 0.0)
    runs = [total_in[a * slice_rows : (a + 1) * slice_rows] * second for a in range(2)]
    for i in range(zs):
        z = order(i)
        for a in range(2):
            rows = slice(a * slice_rows, (a + 1) * slice_rows)
            scan_out[z, rows] = scan_out[z, rows] + runs[a]
            gain = slice_in[z, 2 * slice_rows + a * 4 : 2 * slice_rows + a * 4 + 1]
            runs[a] = gain * runs[a]
    back_in[z_me] = scan_out[z_me]
    returned = z_copies(lambda z: scan_out.at[z], back_in.at[z_me], z_sems.at[2], z_sems.at[3])
    inside(3)
    returned()
    for a in range(2):
        for k in range(2):
            rows = slice(a * 256 + k * 128, a * 256 + (k + 1) * 128)
            slices = slice(k * (zs // 2), (k + 1) * (zs // 2))
            enter = back_in[slices, a * slice_rows : (a + 1) * slice_rows].reshape(128, 128)
            entering[core, rows] = enter
            next_out[rows] = gain_of(mine, a, k) * enter + mine[rows]
    passed = remote(next_out, entering.at[core], pair_sems.at[4], pair_sems.at[5], "seq", core_peer)
    passed.start()

    pick = jnp.where(iota((8, 512), 0) == iota((8, 512), 1) // 64, 1.0, 0.0)
    pick_bf = pick.astype(BF16)
    pick2_bf = jnp.where(iota((8, 256), 0) % 4 == iota((8, 256), 1) // 64, 1.0, 0.0).astype(BF16)
    ones_bf = jnp.ones((8, 128), BF16)

    def same_place(c, carry):
        span = pl.ds(pl.multiple_of(c * Q, Q), Q)
        bc_prod = split2(b_ref[span, :].astype(F32) * c_ref[span, :].astype(F32))
        score8 = dot_nt(ones_bf, bc_prod[0]) + dot_nt(ones_bf, bc_prod[1])
        xg = split2(x_ref[span, :].astype(F32) * g_ref[span, :].astype(F32))
        pair8 = dot_nt(pick2_bf, xg[0]) + dot_nt(pick2_bf, xg[1])
        other_ref[:, span] = score8 * pair8
        return carry

    lax.fori_loop(0, chunks, same_place, 0)
    passed.wait()


    def incoming(q):
        at = (q % 2) * 256
        return jnp.concatenate([entering[q // 2, at + k * 128 : at + (k + 1) * 128] for k in range(2)], axis=1)

    for q, (terms, lanes, way) in enumerate(quantities):
        target = states if terms is ends_ref else adjoints
        run = incoming(q)
        for c in way:
            target[c, :, lanes] = run
            run = run * gain_ref[c, 0:1, lanes] + terms[c, :, lanes]
        if target is states:
            target[chunks, :, lanes] = run

    sent = []
    for c in range(chunks):
        span = slice(c * Q, (c + 1) * Q)
        state_hi, state_lo = split2(states[c])
        adj_hi, adj_lo = split2(adjoints[c])
        xhi, xlo, ghi, glo = xhi_ref[span, :], xlo_ref[span, :], ghi_ref[span, :], glo_ref[span, :]
        db = dot_nt(xhi, adj_hi) + dot_nt(xlo, adj_hi) + dot_nt(xhi, adj_lo)
        dc = dot_nt(ghi, state_hi) + dot_nt(glo, state_hi) + dot_nt(ghi, state_lo)
        part[c, :, :, 0:128] = part[c, :, :, 0:128] + db.reshape(nh, part_rows, 128)
        part[c, :, :, 128:256] = part[c, :, :, 128:256] + dc.reshape(nh, part_rows, 128)
        sent.append(
            head_copies(
                lambda peer, c=c: part.at[c, peer], got.at[c, head_me], head_sems.at[0, c], head_sems.at[1, c]
            )
        )

    def across(c, carry):
        span = pl.ds(pl.multiple_of(c * Q, Q), Q)
        state_hi, state_lo = split2(states[c])
        adj_hi, adj_lo = split2(adjoints[c])
        bc, cc = b_ref[span, :], c_ref[span, :]
        v = dot(bc, adj_hi) + dot(bc, adj_lo)
        y = dot(cc, state_hi) + dot(cc, state_lo)
        scaled = el_ref[span, :] * v
        dx_ref[span, :] = dx_ref[span, :] + scaled[:, FRONT] + scaled[:, MIRROR]
        x_prod = split2((xhi_ref[span, :].astype(F32) + xlo_ref[span, :].astype(F32)) * v)
        g_prod = split2((ghi_ref[span, :].astype(F32) + glo_ref[span, :].astype(F32)) * y)
        col8 = col_keep[c] + dot_nt(pick_bf, x_prod[0]) + dot_nt(pick_bf, x_prod[1])
        row8 = row_keep[c] + dot_nt(pick_bf, g_prod[0]) + dot_nt(pick_bf, g_prod[1])
        s8 = jnp.concatenate([rows_ref[c, 0, 12:16, :], rows_ref[c, 1, 12:16, :]], axis=0)
        step8 = col8 / s8 + other_ref[:, span]
        flow_f = jnp.sum(states[c + 1, :, FRONT] * adjoints[c, :, FRONT], axis=0, keepdims=True)
        under = lax.rem(c + chunks, chunks + 1)
        flow_m = jnp.sum(states[under, :, MIRROR] * adjoints[c, :, MIRROR], axis=0, keepdims=True)
        flow8 = jnp.sum(pick * jnp.concatenate([flow_f, flow_m], axis=1), axis=1, keepdims=True)
        diff = split3(row8 - col8)
        front8 = iota((8, Q), 0) < 4
        decay8 = jnp.where(front8, dot_sum(diff, low_one), dot_sum(diff, up_one)) + flow8
        own_ref[0:4, span] = step8[0:4]
        own_ref[4:8, span] = decay8[0:4]
        other_ref[0:4, span] = step8[4:8]
        other_ref[4:8, span] = decay8[4:8]
        return carry

    def add_up(c):
        sent[c]()
        total = part[c, head_me]
        for k in range(1, nh):
            total = total + got[c, lax.rem(head_me + k, nh)]
        sums_ref[c, head_me] = total
        return head_copies(
            lambda peer: sums_ref.at[c, head_me], sums_ref.at[c, head_me], head_sems.at[2, c], head_sems.at[3, c]
        )

    lax.fori_loop(0, chunks, across, 0)
    others[head_me] = other_ref[...]
    shared = head_copies(lambda peer: other_ref, others.at[head_me], other_sems.at[0], other_sems.at[1])
    ended = [add_up(c) for c in range(chunks)]
    shared()
    for h in range(4):
        place = 0 * head_me
        for k in range(nh * 4):
            place = jnp.where(heads_ref[k] == head_me * 4 + h, k, place)
        dstep_ref[h : h + 1, :] = own_ref[h : h + 1, :] + others[place // 4, pl.ds(place % 4, 1), :]
        ddecay_ref[h : h + 1, :] = own_ref[4 + h : 5 + h, :] + others[place // 4, pl.ds(place % 4 + 4, 1), :]
    for wait in ended:
        wait()


def hand_on(dx_ref, sums_ref, step_ref, decay_ref, dx_out, db_out, dc_out, step_out, decay_out, sems):
    copies = [
        (dx_ref, dx_out),
        (sums_ref.at[:, 0:128], db_out),
        (sums_ref.at[:, 128:256], dc_out),
        (step_ref, step_out),
        (decay_ref, decay_out),
    ]
    started = [pltpu.make_async_copy(a, b, sems.at[i]) for i, (a, b) in enumerate(copies)]
    for copy in started:
        copy.start()
    for copy in started:
        copy.wait()


def on_device(signal, write_keys, read_queries, step_sizes, log_decay, mirror_heads, contig_starts, out_grad):
    nh, ns = lax.axis_size("head"), lax.axis_size("seq")
    length = signal.shape[0]
    chunks = length // Q
    zs = ns // 4
    slice_rows = 256 // zs
    part_rows = Q // nh
    vmem = pl.BlockSpec(memory_space=pltpu.VMEM)
    smem = pl.BlockSpec(memory_space=pltpu.SMEM)
    hbm = pl.BlockSpec(memory_space=pl.ANY)

    def shape(*dims, dtype=F32):
        return jax.ShapeDtypeStruct(dims, dtype)

    def room(*dims, dtype=F32):
        return pltpu.VMEM(dims, dtype)

    dx, sums, dstep, ddecay = pl.pallas_call(
        functools.partial(kernel, nh, ns),
        out_shape=[shape(length, 256), shape(chunks, nh, part_rows, 256), shape(4, length), shape(4, length)],
        in_specs=[smem] * 2 + [vmem] * 6,
        out_specs=[vmem] * 4,
        scratch_shapes=[
            room(nh, 8, length),
            room(chunks, 2, 16, Q),
            room(2, length, 16),
            room(length, 512, dtype=BF16),
            room(length, 512, dtype=BF16),
            room(length, 512, dtype=BF16),
            room(length, 512, dtype=BF16),
            room(length, 512),
            room(chunks, 128, 512),
            room(chunks, 128, 512),
            room(chunks, 8, 512),
            room(2, 544, 128),
            room(544, 128),
            room(zs, 2 * slice_rows + 8, 128),
            room(zs, 2 * slice_rows + 8, 128),
            room(zs, 2 * slice_rows, 128),
            room(2 * slice_rows, 128),
            room(2 * slice_rows, 128),
            room(zs, 2 * slice_rows, 128),
            room(512, 128),
            room(2, 512, 128),
            room(chunks + 1, 128, 512),
            room(chunks, 128, 512),
            room(Q, Q),
            room(4, Q, Q),
            room(4, Q, Q, dtype=BF16),
            room(4, Q, Q, dtype=BF16),
            room(Q, Q, dtype=BF16),
            room(Q, Q, dtype=BF16),
            room(Q, 128),
            room(chunks, 8, Q),
            room(chunks, 8, Q),
            room(chunks, nh, part_rows, 256),
            room(chunks, nh, part_rows, 256),
            room(8, length),
            room(8, length),
            room(nh, 8, length),
            pltpu.SemaphoreType.DMA((2, nh)),
            pltpu.SemaphoreType.DMA((6,)),
            pltpu.SemaphoreType.DMA((4, zs)),
            pltpu.SemaphoreType.DMA((4, chunks, nh)),
            pltpu.SemaphoreType.DMA((2, nh)),
        ],
        compiler_params=pltpu.CompilerParams(
            vmem_limit_bytes=VMEM_LIMIT, collective_id=0, has_side_effects=True
        ),
        name="mixer_backward",
    )(mirror_heads, contig_starts, signal, out_grad, write_keys, read_queries, step_sizes, log_decay)

    return pl.pallas_call(
        hand_on,
        out_shape=[shape(length, 256), shape(length, 128), shape(length, 128), shape(4, length), shape(4, length)],
        in_specs=[hbm] * 4,
        out_specs=[hbm] * 5,
        scratch_shapes=[pltpu.SemaphoreType.DMA((5,))],
        name="hand_on",
    )(dx, sums.reshape(length, 256), dstep, ddecay)


def solution(mesh):
    return jax.shard_map(
        on_device,
        mesh=mesh,
        in_specs=(
            P("seq", "head"),
            P("seq", None),
            P("seq", None),
            P("head", "seq"),
            P("head", "seq"),
            P(),
            P(),
            P("seq", "head"),
        ),
        out_specs=(
            P("seq", "head"),
            P("seq", None),
            P("seq", None),
            P("head", "seq"),
            P("head", "seq"),
        ),
        check_vma=False,
    )
```

time: 1000 us -> 144 us (0.14)
  waiting for transfers between devices: 341 us -> 0 us
  local copies, waits for them, and re-layouts: 213 us -> 0 us
  starting transfers between devices: 149 us -> 0 us
  Pallas kernels: 0 us -> 143 us
  other arithmetic: 139 us -> 0 us
  matrix products: 81.8 us -> 0 us
  blocking collectives: 45 us -> 0 us
  between operations: 16.4 us -> 0.64 us
    ppermute x62 -> x0, waiting for transfers between devices: 250 us -> none  [shifted(): lax.ppermute(value, axis, [(source, source + steps) for source in range(l...]
    ppermute x62 -> x0, starting transfers between devices: 149 us -> none  [shifted(): lax.ppermute(value, axis, [(source, source + steps) for source in range(l...]
    pallas_call x0 -> x2, Pallas kernels: none -> 143 us  [the longest x1 77.7 us: on_device(): pl.pallas_call(functools.partial(kernel, nh, ns), out_shape=[shape(length...]
    psum x1 -> x0, waiting for transfers between devices: 91.3 us -> none  [on_device(): write_grad, read_grad = lax.psum((gradients[1], gradients[2]), 'head')]
    dot_general x96 -> x0, matrix products: 81.8 us -> none  [the longest x16 27.7 us: block_step(): inside = jnp.einsum('hts,shp->thp', weights, values, precision=highest)]
    dynamic_update_slice x40 -> x0, local copies, waits for them, and re-layouts: 64.5 us -> none  [strand(): lax.scan(jax.checkpoint(block_step), (state_in, seg_before), blocks)]
    another operation x62 -> x0, other arithmetic: 63.8 us -> none
    all_gather x2 -> x0, blocking collectives: 45 us -> none  [the longest x1 23.2 us: on_device(): lax.all_gather(step_sizes, 'head', axis=0, tiled=True)]
  transfers between devices with their start and end apart: 63 -> 0, of which waited for: 63 -> 0; matrix products, arithmetic and copies ran while one was open for 1% -> 0% of each run, Pallas kernels for 0% -> 0%
where the time goes in v1:
time: 144 us
  Pallas kernels  143 us (99%)
    pallas_call x1, Pallas kernels, on_device(): pl.pallas_call(functools.partial(kernel, nh, ns), out_shape=[shape(length...  77.7 us
    pallas_call x1, Pallas kernels, on_device(): pl.pallas_call(hand_on, out_shape=[shape(length, 256), shape(length, 128)...  65.7 us

profile of v1, /device:TPU:1, one launch (start us, length us, event | category | flops | bytes accessed | tf_op | source)
XLA Modules:
  0.0 144.0 jit_solution(11681779129910916901)
XLA Ops:
  0.6 77.7 %mixer_backward.1 = (f32[1024,256]{1,0:T(8,128)}, f32[4,8,32,256]{3,2,1,0:T(8,128)}, f32[4,1024]{1,0:T(4,128)}, f32[4,1024]{1,0:T(4,128)}) custom-call(s32[32]{0:T(128)} %heads_ref.1, s32[4]{0:T(128)} %starts_ref.1, bf16[1024,256]{1,0:T(8,128)(2,1)} %x_ref.1, bf16[1024,256]{1,0:T(8,128)(2,1)} %g_ref.1, bf16[1024,128]{1,0:T(8,128)(2,1)} %b_ref.1, ...), custom_call_target="tpu_custom_call" | custom-call | tf_op jit(solution)/shard_map/mixer_backward/pallas_call | solution.py:587
  78.4 65.7 %hand_on.1 = (f32[1024,256]{1,0:T(8,128)}, f32[1024,128]{1,0:T(8,128)}, f32[1024,128]{1,0:T(8,128)}, f32[4,1024]{1,0:T(4,128)}, f32[4,1024]{1,0:T(4,128)}) custom-call(f32[1024,256]{1,0:T(8,128)} %get-tuple-element.9.dx_ref, f32[1024,256]{1,0:T(8,128)} %bitcast.1, f32[4,1024]{1,0:T(4,128)} %get-tuple-element.11.step_ref, f32[4,1024]{1,0:T(4,128)} %get-tuple-element.12.decay_ref), custom_call_target="tpu_custom_call" | custom-call | tf_op jit(solution)/shard_map/hand_on/pallas_call | solution.py:642

commit v2 on v1

--- a/solution.py
+++ b/solution.py
@@ -219,11 +219,10 @@
             seg = segment_at(starts_ref, first + iota((8, Q), 1))
             seg_first, seg_last = segment_at(starts_ref, first), segment_at(starts_ref, first + Q - 1)
             if strand:
-                seg_in, seg_near, seg_far = segment_at(starts_ref, first + Q), seg_last, seg_first
+                seg_in, seg_far = segment_at(starts_ref, first + Q), seg_first
             else:
                 seg_in = jnp.where(first == 0, -1, segment_at(starts_ref, first - 1))
-                seg_near, seg_far = seg_first, seg_last
-            del seg_near
+                seg_far = seg_last
             e8 = jnp.where(seg == seg_in, jnp.exp2(cum8), 0.0)
             l8 = jnp.where(seg == seg_far, jnp.exp2(total8 - cum8) * s8, 0.0)
             gain8 = jnp.exp2(total8) * (seg_in == seg_far).astype(F32)
@@ -552,19 +551,12 @@
         wait()
 
 
-def hand_on(dx_ref, sums_ref, step_ref, decay_ref, dx_out, db_out, dc_out, step_out, decay_out, sems):
-    copies = [
-        (dx_ref, dx_out),
-        (sums_ref.at[:, 0:128], db_out),
-        (sums_ref.at[:, 128:256], dc_out),
-        (step_ref, step_out),
-        (decay_ref, decay_out),
-    ]
-    started = [pltpu.make_async_copy(a, b, sems.at[i]) for i, (a, b) in enumerate(copies)]
-    for copy in started:
-        copy.start()
-    for copy in started:
-        copy.wait()
+def hand_on(dx_ref, sums_ref, step_ref, decay_ref, dx_out, db_out, dc_out, step_out, decay_out):
+    dx_out[...] = dx_ref[...]
+    db_out[...] = sums_ref[:, 0:128]
+    dc_out[...] = sums_ref[:, 128:256]
+    step_out[...] = step_ref[...]
+    decay_out[...] = decay_ref[...]
 
 
 def on_device(signal, write_keys, read_queries, step_sizes, log_decay, mirror_heads, contig_starts, out_grad):
@@ -576,7 +568,10 @@
     part_rows = Q // nh
     vmem = pl.BlockSpec(memory_space=pltpu.VMEM)
     smem = pl.BlockSpec(memory_space=pltpu.SMEM)
-    hbm = pl.BlockSpec(memory_space=pl.ANY)
+    across_lanes = pl.BlockSpec((4, Q), lambda i: (0, i))
+
+    def across_rows(width):
+        return pl.BlockSpec((Q, width), lambda i: (i, 0))
 
     def shape(*dims, dtype=F32):
         return jax.ShapeDtypeStruct(dims, dtype)
@@ -642,9 +637,9 @@
     return pl.pallas_call(
         hand_on,
         out_shape=[shape(length, 256), shape(length, 128), shape(length, 128), shape(4, length), shape(4, length)],
-        in_specs=[hbm] * 4,
-        out_specs=[hbm] * 5,
-        scratch_shapes=[pltpu.SemaphoreType.DMA((5,))],
+        grid=(chunks,),
+        in_specs=[across_rows(256)] * 2 + [across_lanes] * 2,
+        out_specs=[across_rows(256), across_rows(128), across_rows(128)] + [across_lanes] * 2,
         name="hand_on",
     )(dx, sums.reshape(length, 256), dstep, ddecay)
 

time: 144 us -> 82.3 us (0.57)
  Pallas kernels: 143 us -> 81.5 us
    pallas_call x1, Pallas kernels: 65.7 us -> 3.77 us  [on_device(): pl.pallas_call(hand_on, out_shape=[shape(length, 256), shape(length, 128)...]
where the time goes in v2:
time: 82.3 us; the launch traced here: 82.1 us
  Pallas kernels  81.5 us (99%)
    pallas_call x1, Pallas kernels, on_device(): pl.pallas_call(functools.partial(kernel, nh, ns), out_shape=[shape(length...  77.7 us
    pallas_call x1, Pallas kernels, on_device(): pl.pallas_call(hand_on, out_shape=[shape(length, 256), shape(length, 128)...  3.77 us

profile of v2, /device:TPU:1, one launch (start us, length us, event | category | flops | bytes accessed | tf_op | source)
XLA Modules:
  0.0 82.1 jit_solution(7140028531698201699)
XLA Ops:
  0.6 77.7 %mixer_backward.1 = (f32[1024,256]{1,0:T(8,128)}, f32[4,8,32,256]{3,2,1,0:T(8,128)}, f32[4,1024]{1,0:T(4,128)}, f32[4,1024]{1,0:T(4,128)}) custom-call(s32[32]{0:T(128)} %heads_ref.1, s32[4]{0:T(128)} %starts_ref.1, bf16[1024,256]{1,0:T(8,128)(2,1)} %x_ref.1, bf16[1024,256]{1,0:T(8,128)(2,1)} %g_ref.1, bf16[1024,128]{1,0:T(8,128)(2,1)} %b_ref.1, ...), custom_call_target="tpu_custom_call" | custom-call | tf_op jit(solution)/shard_map/mixer_backward/pallas_call | solution.py:582
  78.4 3.8 %hand_on.1 = (f32[1024,256]{1,0:T(8,128)}, f32[1024,128]{1,0:T(8,128)}, f32[1024,128]{1,0:T(8,128)}, f32[4,1024]{1,0:T(4,128)}, f32[4,1024]{1,0:T(4,128)}) custom-call(f32[1024,256]{1,0:T(8,128)} %get-tuple-element.9.dx_ref, f32[1024,256]{1,0:T(8,128)} %bitcast.1, f32[4,1024]{1,0:T(4,128)} %get-tuple-element.11.step_ref, f32[4,1024]{1,0:T(4,128)} %get-tuple-element.12.decay_ref), custom_call_target="tpu_custom_call" | custom-call | tf_op jit(solution)/shard_map/hand_on/pallas_call | solution.py:637

commit v3 on v2

--- a/solution.py
+++ b/solution.py
@@ -109,6 +109,8 @@
     own_ref,
     other_ref,
     others,
+    far_out,
+    far_in,
     gather_sems,
     pair_sems,
     z_sems,
@@ -248,32 +250,28 @@
 
         lax.fori_loop(0, chunks, chunk, 0)
 
-    prepare(0)
-    gathered()
-    prepare(1)
-
-    whole = gain_ref[0]
-    for c in range(1, chunks):
-        whole = whole * gain_ref[c]
+
     ascending, descending = range(chunks), range(chunks - 1, -1, -1)
-    quantities = (
-        (ends_ref, FRONT, ascending),
-        (seeds_ref, MIRROR, ascending),
-        (ends_ref, MIRROR, descending),
-        (seeds_ref, FRONT, descending),
-    )
-    for q, (terms, lanes, order) in enumerate(quantities):
-        run = None
-        for c in order:
-            run = terms[c, :, lanes] if run is None else run * gain_ref[c, 0:1, lanes] + terms[c, :, lanes]
-        for k in range(2):
-            pair_out[q // 2, (q % 2) * 256 + k * 128 : (q % 2) * 256 + (k + 1) * 128] = run[:, k * 128 : (k + 1) * 128]
-    for p in range(2):
-        for a in range(2):
-            lanes = STRANDS[(p + a) % 2]
-            gains = whole[:, lanes]
+    way = (ascending, descending)
+
+    def terms_of(strand, d):
+        return (ends_ref, seeds_ref)[(strand + d) % 2]
+
+    def fold(strand):
+        lanes = STRANDS[strand]
+        for d in range(2):
+            run = None
+            for c in way[d]:
+                term = terms_of(strand, d)[c, :, lanes]
+                run = term if run is None else run * gain_ref[c, 0:1, lanes] + term
             for k in range(2):
-                pair_out[p, 512 + (a * 2 + k) * 8 : 512 + (a * 2 + k + 1) * 8] = gains[:, k * 128 : (k + 1) * 128]
+                pair_out[strand, d, k * 128 : (k + 1) * 128] = run[:, k * 128 : (k + 1) * 128]
+        whole = gain_ref[0, :, lanes]
+        for c in range(1, chunks):
+            whole = whole * gain_ref[c, :, lanes]
+        for d in range(2):
+            for k in range(2):
+                pair_out[strand, d, 256 + k * 8 : 264 + k * 8] = whole[:, k * 128 : (k + 1) * 128]
 
 
     half_mask = [jnp.where(iota((1, 128), 1) // 64 == k, 1.0, 0.0).astype(BF16) for k in range(2)]
@@ -283,85 +281,89 @@
     def put_part(c, lanes, value):
         part[c, :, :, lanes] = value.reshape(nh, part_rows, 128)
 
-    def inside(c):
+    kept_sums = {}
+
+    def inside(c, i):
         base = c * Q
         span = slice(base, base + Q)
         first = offset + base
         bc, cc = b_ref[span, :], c_ref[span, :]
         xs = [x_ref[span, k * 128 : (k + 1) * 128] for k in range(2)]
         gs = [g_ref[span, k * 128 : (k + 1) * 128] for k in range(2)]
-        seg_s = segment_at(starts_ref, first + iota((Q, 1), 0))
-        seg_t = segment_at(starts_ref, first + iota((1, Q), 1))
-        gm[...] = jnp.where(seg_s == seg_t, dot_nt(bc, cc), 0.0)
-        for h in range(4):
-            pt[h] = dot_nt(xs[h // 2] * half_mask[h % 2], gs[h // 2])
-        row_sums = []
-        for i in range(2):
-
-            def strip(r, sums, i=i):
-                start = pl.multiple_of(i * 128 + r * STRIP, STRIP)
-                at = pl.ds(start, STRIP)
-                at_cols = pl.ds(pl.multiple_of(base + start, STRIP), STRIP)
-                col_f, col_m = cols_ref[0, at_cols, :], cols_ref[1, at_cols, :]
-                lane128 = iota((STRIP, 128), 1)
-                s_index = r * STRIP + iota((STRIP, 128), 0)
-                ahead = lane128 > s_index
-                behind = lane128 < s_index
-                sums = list(sums)
-                collected = jnp.zeros((STRIP, 128), F32)
-                dg = [jnp.zeros((STRIP, 128), F32) for _ in range(2)]
-                for h in range(4):
-                    cum_f, cum_m = col_f[:, h : h + 1], col_m[:, h : h + 1]
-                    step_f, step_m = col_f[:, 12 + h : 13 + h], col_m[:, 12 + h : 13 + h]
-                    lane_sums = [None, None]
-                    for j in range(2):
-                        t = slice(j * 128, (j + 1) * 128)
-                        row_f = rows_ref[c, 0, h : h + 1, t]
-                        row_m = rows_ref[c, 1, h : h + 1, t]
-                        if i == j:
-                            gap = jnp.where(behind, row_m - cum_m, row_f - cum_f)
-                            step = jnp.where(behind, step_m, jnp.where(ahead, step_f, step_f + step_m))
-                        elif j > i:
-                            gap, step = row_f - cum_f, step_f
-                        else:
-                            gap, step = row_m - cum_m, step_m
-                        d = jnp.exp2(gap) * step
-                        w = d * gm[at, t]
-                        p = pt[h, at, t]
-                        dg[j] = dg[j] + d * p
-                        e = w * p
-                        hi, lo = split2(w)
-                        whi[h, at, t] = hi
-                        wlo[h, at, t] = lo
-                        if i == j:
-                            parts = [jnp.where(ahead, e, 0.0), jnp.where(behind, e, 0.0)]
-                        else:
-                            parts = [e, None] if j > i else [None, e]
-                        for strand in range(2):
-                            piece = parts[strand]
-                            if piece is None:
-                                continue
-                            slot = (h * 2 + j) * 2 + strand
-                            add = piece[0:8]
-                            for u in range(1, STRIP // 8):
-                                add = add + piece[u * 8 : (u + 1) * 8]
-                            sums[slot] = sums[slot] + add
-                            old = lane_sums[strand]
-                            lane_sums[strand] = piece if old is None else old + piece
-                    for strand in range(2):
-                        total = jnp.sum(lane_sums[strand], axis=1, keepdims=True)
-                        collected = jnp.where(lane128 == strand * 4 + h, total, collected)
-                csum[at, :] = collected
-                rows_at = segment_at(starts_ref, first + start + iota((STRIP, 1), 0))
+        if i == 0:
+            seg_s = segment_at(starts_ref, first + iota((Q, 1), 0))
+            seg_t = segment_at(starts_ref, first + iota((1, Q), 1))
+            gm[...] = jnp.where(seg_s == seg_t, dot_nt(bc, cc), 0.0)
+            for h in range(4):
+                pt[h] = dot_nt(xs[h // 2] * half_mask[h % 2], gs[h // 2])
+
+        def strip(r, sums):
+            start = pl.multiple_of(i * 128 + r * STRIP, STRIP)
+            at = pl.ds(start, STRIP)
+            at_cols = pl.ds(pl.multiple_of(base + start, STRIP), STRIP)
+            col_f, col_m = cols_ref[0, at_cols, :], cols_ref[1, at_cols, :]
+            lane128 = iota((STRIP, 128), 1)
+            s_index = r * STRIP + iota((STRIP, 128), 0)
+            ahead = lane128 > s_index
+            behind = lane128 < s_index
+            sums = list(sums)
+            collected = jnp.zeros((STRIP, 128), F32)
+            dg = [jnp.zeros((STRIP, 128), F32) for _ in range(2)]
+            for h in range(4):
+                cum_f, cum_m = col_f[:, h : h + 1], col_m[:, h : h + 1]
+                step_f, step_m = col_f[:, 12 + h : 13 + h], col_m[:, 12 + h : 13 + h]
+                lane_sums = [None, None]
                 for j in range(2):
                     t = slice(j * 128, (j + 1) * 128)
-                    cols_at = segment_at(starts_ref, first + j * 128 + iota((1, 128), 1))
-                    hi, lo = split2(jnp.where(rows_at == cols_at, dg[j], 0.0))
-                    dghi[at, t] = hi
-                    dglo[at, t] = lo
-                return tuple(sums)
-
-            row_sums.append(lax.fori_loop(0, 128 // STRIP, strip, (zero_row,) * 16))
+                    row_f = rows_ref[c, 0, h : h + 1, t]
+                    row_m = rows_ref[c, 1, h : h + 1, t]
+                    if i == j:
+                        gap = jnp.where(behind, row_m - cum_m, row_f - cum_f)
+                        step = jnp.where(behind, step_m, jnp.where(ahead, step_f, step_f + step_m))
+                    elif j > i:
+                        gap, step = row_f - cum_f, step_f
+                    else:
+                        gap, step = row_m - cum_m, step_m
+                    d = jnp.exp2(gap) * step
+                    w = d * gm[at, t]
+                    p = pt[h, at, t]
+                    dg[j] = dg[j] + d * p
+                    e = w * p
+                    hi, lo = split2(w)
+                    whi[h, at, t] = hi
+                    wlo[h, at, t] = lo
+                    if i == j:
+                        parts = [jnp.where(ahead, e, 0.0), jnp.where(behind, e, 0.0)]
+                    else:
+                        parts = [e, None] if j > i else [None, e]
+                    for strand in range(2):
+                        piece = parts[strand]
+                        if piece is None:
+                            continue
+                        slot = (h * 2 + j) * 2 + strand
+                        add = piece[0:8]
+                        for u in range(1, STRIP // 8):
+                            add = add + piece[u * 8 : (u + 1) * 8]
+                        sums[slot] = sums[slot] + add
+                        old = lane_sums[strand]
+                        lane_sums[strand] = piece if old is None else old + piece
+                for strand in range(2):
+                    total = jnp.sum(lane_sums[strand], axis=1, keepdims=True)
+                    collected = jnp.where(lane128 == strand * 4 + h, total, collected)
+            csum[at, :] = collected
+            rows_at = segment_at(starts_ref, first + start + iota((STRIP, 1), 0))
+            for j in range(2):
+                t = slice(j * 128, (j + 1) * 128)
+                cols_at = segment_at(starts_ref, first + j * 128 + iota((1, 128), 1))
+                hi, lo = split2(jnp.where(rows_at == cols_at, dg[j], 0.0))
+                dghi[at, t] = hi
+                dglo[at, t] = lo
+            return tuple(sums)
+
+        kept_sums[i] = lax.fori_loop(0, 128 // STRIP, strip, (zero_row,) * 16)
+        if i == 0:
+            return
+        row_sums = [kept_sums[0], kept_sums[1]]
         rows_in = []
         for strand in range(2):
             for h in range(4):
@@ -385,71 +387,142 @@
 
 
     other = 1 - core
-    trade = remote(pair_out.at[other], pair_in, pair_sems.at[0], pair_sems.at[1], "seq", core_peer)
-    trade.start()
-    inside(0)
-    trade.wait()
-
-    def gain_of(ref, a, k):
-        return ref[512 + (a * 2 + k) * 8 : 512 + (a * 2 + k + 1) * 8][0:1]
-
-    mine = pair_out.at[core]
     slice_rows = 256 // zs
-    for a in range(2):
-        for k in range(2):
-            rows = slice(a * 256 + k * 128, a * 256 + (k + 1) * 128)
-            chip = gain_of(pair_in, a, k) * mine[rows] + pair_in[rows]
-            slices = slice(k * (zs // 2), (k + 1) * (zs // 2))
-            slice_out[slices, a * slice_rows : (a + 1) * slice_rows] = chip.reshape(zs // 2, slice_rows, 128)
-    for k in range(2):
-        gains = [gain_of(pair_in, a, k) * gain_of(mine, a, k) for a in range(2)]
-        both = jnp.where(iota((8, 128), 0) < 4, gains[0], gains[1])
-        slices = slice(k * (zs // 2), (k + 1) * (zs // 2))
-        slice_out[slices, 2 * slice_rows : 2 * slice_rows + 8] = jnp.broadcast_to(both[None], (zs // 2, 8, 128))
-    slice_in[z_me] = slice_out[z_me]
-    sliced = z_copies(lambda z: slice_out.at[z], slice_in.at[z_me], z_sems.at[0], z_sems.at[1])
-    inside(1)
-    sliced()
+    half_slices = zs // 2
+    waits = {}
+
+    def gain_of(ref, k):
+        return ref[256 + k * 8 : 257 + k * 8]
 
     def order(i):
         return i + core * (zs - 1 - 2 * i)
 
-    runs = [jnp.zeros((slice_rows, 128), F32) for _ in range(2)]
-    for i in range(zs):
-        z = order(i)
-        for a in range(2):
-            rows = slice(a * slice_rows, (a + 1) * slice_rows)
-            scan_out[z, rows] = runs[a]
-            gain = slice_in[z, 2 * slice_rows + a * 4 : 2 * slice_rows + a * 4 + 1]
-            runs[a] = gain * runs[a] + slice_in[z, rows]
-    for a in range(2):
-        total_out[a * slice_rows : (a + 1) * slice_rows] = runs[a]
-    swap = remote(total_out, total_in, pair_sems.at[2], pair_sems.at[3], "seq", x_peer)
-    swap.start()
-    inside(2)
-    swap.wait()
-    second = jnp.where(x_me == 1 - core, 1.0, 0.0)
-    runs = [total_in[a * slice_rows : (a + 1) * slice_rows] * second for a in range(2)]
-    for i in range(zs):
-        z = order(i)
-        for a in range(2):
-            rows = slice(a * slice_rows, (a + 1) * slice_rows)
-            scan_out[z, rows] = scan_out[z, rows] + runs[a]
-            gain = slice_in[z, 2 * slice_rows + a * 4 : 2 * slice_rows + a * 4 + 1]
-            runs[a] = gain * runs[a]
-    back_in[z_me] = scan_out[z_me]
-    returned = z_copies(lambda z: scan_out.at[z], back_in.at[z_me], z_sems.at[2], z_sems.at[3])
-    inside(3)
-    returned()
-    for a in range(2):
+    def trade(strand):
+        fold(strand)
+        copy = remote(
+            pair_out.at[strand, other],
+            pair_in.at[strand],
+            pair_sems.at[strand, 0],
+            pair_sems.at[strand, 1],
+            "seq",
+            core_peer,
+        )
+        copy.start()
+        waits["trade", strand] = copy.wait
+
+    def spread_chip(strand):
+        waits["trade", strand]()
+        mine, theirs = pair_out.at[strand, core], pair_in.at[strand]
         for k in range(2):
-            rows = slice(a * 256 + k * 128, a * 256 + (k + 1) * 128)
-            slices = slice(k * (zs // 2), (k + 1) * (zs // 2))
-            enter = back_in[slices, a * slice_rows : (a + 1) * slice_rows].reshape(128, 128)
-            entering[core, rows] = enter
-            next_out[rows] = gain_of(mine, a, k) * enter + mine[rows]
-    passed = remote(next_out, entering.at[core], pair_sems.at[4], pair_sems.at[5], "seq", core_peer)
-    passed.start()
+            rows = slice(k * 128, (k + 1) * 128)
+            slices = slice(k * half_slices, (k + 1) * half_slices)
+            chip = gain_of(theirs, k) * mine[rows] + theirs[rows]
+            slice_out[strand, slices, 0:slice_rows] = chip.reshape(half_slices, slice_rows, 128)
+            gain = gain_of(theirs, k) * gain_of(mine, k)
+            slice_out[strand, slices, slice_rows : slice_rows + 8] = jnp.broadcast_to(
+                gain[None], (half_slices, 8, 128)
+            )
+        slice_in[strand, z_me] = slice_out[strand, z_me]
+        waits["spread", strand] = z_copies(
+            lambda z: slice_out.at[strand, z], slice_in.at[strand, z_me], z_sems.at[strand, 0], z_sems.at[strand, 1]
+        )
+
+    def scan_half(strand):
+        waits["spread", strand]()
+        run = jnp.zeros((slice_rows, 128), F32)
+        for i in range(zs):
+            z = order(i)
+            scan_out[strand, z] = run
+            run = slice_in[strand, z, slice_rows : slice_rows + 1] * run + slice_in[strand, z, 0:slice_rows]
+        total_out[strand] = run
+        copy = remote(
+            total_out.at[strand],
+            total_in.at[strand],
+            pair_sems.at[strand, 2],
+            pair_sems.at[strand, 3],
+            "seq",
+            x_peer,
+        )
+        copy.start()
+        waits["swap", strand] = copy.wait
+
+    def send_back(strand):
+        waits["swap", strand]()
+        run = total_in[strand] * jnp.where(x_me == 1 - core, 1.0, 0.0)
+        for i in range(zs):
+            z = order(i)
+            scan_out[strand, z] = scan_out[strand, z] + run
+            run = slice_in[strand, z, slice_rows : slice_rows + 1] * run
+        back_in[strand, z_me] = scan_out[strand, z_me]
+        waits["back", strand] = z_copies(
+            lambda z: scan_out.at[strand, z], back_in.at[strand, z_me], z_sems.at[strand, 2], z_sems.at[strand, 3]
+        )
+
+    def pass_on(strand):
+        waits["back", strand]()
+        mine = pair_out.at[strand, core]
+        for k in range(2):
+            rows = slice(k * 128, (k + 1) * 128)
+            enter = back_in[strand, k * half_slices : (k + 1) * half_slices].reshape(128, 128)
+            entering[strand, core, rows] = enter
+            next_out[strand, rows] = gain_of(mine, k) * enter + mine[rows]
+        copy = remote(
+            next_out.at[strand],
+            entering.at[strand, core],
+            pair_sems.at[strand, 4],
+            pair_sems.at[strand, 5],
+            "seq",
+            core_peer,
+        )
+        copy.start()
+        waits["pass", strand] = copy.wait
+
+    def enter_chunks(strand):
+        waits["pass", strand]()
+        lanes = STRANDS[strand]
+        for d in range(2):
+            terms = terms_of(strand, d)
+            target = states if terms is ends_ref else adjoints
+            run = jnp.concatenate([entering[strand, d, k * 128 : (k + 1) * 128] for k in range(2)], axis=1)
+            for c in way[d]:
+                target[c, :, lanes] = run
+                run = run * gain_ref[c, 0:1, lanes] + terms[c, :, lanes]
+            if target is states:
+                target[chunks, :, lanes] = run
+
+    def cross(c, strand):
+        span = slice(c * Q, (c + 1) * Q)
+        lanes = STRANDS[strand]
+        state_hi, state_lo = split2(states[c, :, lanes])
+        adj_hi, adj_lo = split2(adjoints[c, :, lanes])
+        xhi, xlo, ghi, glo = xhi_ref[span, lanes], xlo_ref[span, lanes], ghi_ref[span, lanes], glo_ref[span, lanes]
+        db = dot_nt(xhi, adj_hi) + dot_nt(xlo, adj_hi) + dot_nt(xhi, adj_lo)
+        dc = dot_nt(ghi, state_hi) + dot_nt(glo, state_hi) + dot_nt(ghi, state_lo)
+        part[c, :, :, 0:128] = part[c, :, :, 0:128] + db.reshape(nh, part_rows, 128)
+        part[c, :, :, 128:256] = part[c, :, :, 128:256] + dc.reshape(nh, part_rows, 128)
+
+    prepare(0)
+    trade(0)
+    gathered()
+    spread_chip(0)
+    prepare(1)
+    trade(1)
+    scan_half(0)
+    inside(0, 0)
+    spread_chip(1)
+    inside(0, 1)
+    send_back(0)
+    inside(1, 0)
+    inside(1, 1)
+    scan_half(1)
+    inside(2, 0)
+    pass_on(0)
+    inside(2, 1)
+    send_back(1)
+    inside(3, 0)
+    inside(3, 1)
+    enter_chunks(0)
+    pass_on(1)
 
     pick = jnp.where(iota((8, 512), 0) == iota((8, 512), 1) // 64, 1.0, 0.0)
     pick_bf = pick.astype(BF16)
@@ -466,32 +539,13 @@
         return carry
 
     lax.fori_loop(0, chunks, same_place, 0)
-    passed.wait()
-
-
-    def incoming(q):
-        at = (q % 2) * 256
-        return jnp.concatenate([entering[q // 2, at + k * 128 : at + (k + 1) * 128] for k in range(2)], axis=1)
-
-    for q, (terms, lanes, way) in enumerate(quantities):
-        target = states if terms is ends_ref else adjoints
-        run = incoming(q)
-        for c in way:
-            target[c, :, lanes] = run
-            run = run * gain_ref[c, 0:1, lanes] + terms[c, :, lanes]
-        if target is states:
-            target[chunks, :, lanes] = run
+    for c in range(chunks):
+        cross(c, 0)
+    enter_chunks(1)
 
     sent = []
     for c in range(chunks):
-        span = slice(c * Q, (c + 1) * Q)
-        state_hi, state_lo = split2(states[c])
-        adj_hi, adj_lo = split2(adjoints[c])
-        xhi, xlo, ghi, glo = xhi_ref[span, :], xlo_ref[span, :], ghi_ref[span, :], glo_ref[span, :]
-        db = dot_nt(xhi, adj_hi) + dot_nt(xlo, adj_hi) + dot_nt(xhi, adj_lo)
-        dc = dot_nt(ghi, state_hi) + dot_nt(glo, state_hi) + dot_nt(ghi, state_lo)
-        part[c, :, :, 0:128] = part[c, :, :, 0:128] + db.reshape(nh, part_rows, 128)
-        part[c, :, :, 128:256] = part[c, :, :, 128:256] + dc.reshape(nh, part_rows, 128)
+        cross(c, 1)
         sent.append(
             head_copies(
                 lambda peer, c=c: part.at[c, peer], got.at[c, head_me], head_sems.at[0, c], head_sems.at[1, c]
@@ -537,16 +591,42 @@
         )
 
     lax.fori_loop(0, chunks, across, 0)
-    others[head_me] = other_ref[...]
-    shared = head_copies(lambda peer: other_ref, others.at[head_me], other_sems.at[0], other_sems.at[1])
-    ended = [add_up(c) for c in range(chunks)]
+    ny = nh // 2
+    y_me, side = lax.rem(head_me, ny), head_me // ny
+    x_head = lax.rem(head_me + ny, nh)
+    others[y_me] = other_ref[...]
+
+    def y_copy(k):
+        peer = side * ny + lax.rem(y_me + k, ny)
+        return remote(other_ref, others.at[y_me], other_sems.at[0, k], other_sems.at[1, k], "head", peer)
+
+    shared = every(ny, y_copy)
+
+    def find(head):
+        place = 0 * head
+        for k in range(nh * 4):
+            place = jnp.where(heads_ref[k] == head, k, place)
+        return place
+
+    def row_of(place, row):
+        return others[lax.rem(place // 4, ny), pl.ds(lax.rem(place, 4) + row, 1), :]
+
+    ended = [add_up(c) for c in range(chunks // 2)]
     shared()
     for h in range(4):
-        place = 0 * head_me
-        for k in range(nh * 4):
-            place = jnp.where(heads_ref[k] == head_me * 4 + h, k, place)
-        dstep_ref[h : h + 1, :] = own_ref[h : h + 1, :] + others[place // 4, pl.ds(place % 4, 1), :]
-        ddecay_ref[h : h + 1, :] = own_ref[4 + h : 5 + h, :] + others[place // 4, pl.ds(place % 4 + 4, 1), :]
+        place = find(x_head * 4 + h)
+        far_out[h : h + 1, :] = row_of(place, 0)
+        far_out[4 + h : 5 + h, :] = row_of(place, 4)
+    far = remote(far_out, far_in, other_sems.at[0, 0], other_sems.at[1, 0], "head", x_head)
+    far.start()
+    ended += [add_up(c) for c in range(chunks // 2, chunks)]
+    far.wait()
+    for h in range(4):
+        place = find(head_me * 4 + h)
+        near = place // (4 * ny) == side
+        for row, target in ((0, dstep_ref), (4, ddecay_ref)):
+            back = jnp.where(near, row_of(place, row), far_in[row + h : row + h + 1, :])
+            target[h : h + 1, :] = own_ref[row + h : row + h + 1, :] + back
     for wait in ended:
         wait()
 
@@ -596,16 +676,16 @@
             room(chunks, 128, 512),
             room(chunks, 128, 512),
             room(chunks, 8, 512),
-            room(2, 544, 128),
-            room(544, 128),
-            room(zs, 2 * slice_rows + 8, 128),
-            room(zs, 2 * slice_rows + 8, 128),
-            room(zs, 2 * slice_rows, 128),
-            room(2 * slice_rows, 128),
-            room(2 * slice_rows, 128),
-            room(zs, 2 * slice_rows, 128),
-            room(512, 128),
-            room(2, 512, 128),
+            room(2, 2, 272, 128),
+            room(2, 272, 128),
+            room(2, zs, slice_rows + 8, 128),
+            room(2, zs, slice_rows + 8, 128),
+            room(2, zs, slice_rows, 128),
+            room(2, slice_rows, 128),
+            room(2, slice_rows, 128),
+            room(2, zs, slice_rows, 128),
+            room(2, 256, 128),
+            room(2, 2, 256, 128),
             room(chunks + 1, 128, 512),
             room(chunks, 128, 512),
             room(Q, Q),
@@ -621,10 +701,12 @@
             room(chunks, nh, part_rows, 256),
             room(8, length),
             room(8, length),
-            room(nh, 8, length),
+            room(nh // 2, 8, length),
+            room(8, length),
+            room(8, length),
             pltpu.SemaphoreType.DMA((2, nh)),
-            pltpu.SemaphoreType.DMA((6,)),
-            pltpu.SemaphoreType.DMA((4, zs)),
+            pltpu.SemaphoreType.DMA((2, 6)),
+            pltpu.SemaphoreType.DMA((2, 4, zs)),
             pltpu.SemaphoreType.DMA((4, chunks, nh)),
             pltpu.SemaphoreType.DMA((2, nh)),
         ],

time: 82.3 us -> 77.6 us (0.943)
  Pallas kernels: 81.5 us -> 76.7 us
    pallas_call x1, Pallas kernels: 77.7 us -> 73 us  [on_device(): pl.pallas_call(functools.partial(kernel, nh, ns), out_shape=[shape(length...]
where the time goes in v3:
time: 77.6 us; the launch traced here: 77.4 us
  Pallas kernels  76.7 us (99%)
    pallas_call x1, Pallas kernels, on_device(): pl.pallas_call(functools.partial(kernel, nh, ns), out_shape=[shape(length...  73 us
    pallas_call x1, Pallas kernels, on_device(): pl.pallas_call(hand_on, out_shape=[shape(length, 256), shape(length, 128)...  3.77 us

profile of v3, /device:TPU:1, one launch (start us, length us, event | category | flops | bytes accessed | tf_op | source)
XLA Modules:
  0.0 77.4 jit_solution(14919544170426016151)
XLA Ops:
  0.6 73.0 %mixer_backward.1 = (f32[1024,256]{1,0:T(8,128)}, f32[4,8,32,256]{3,2,1,0:T(8,128)}, f32[4,1024]{1,0:T(4,128)}, f32[4,1024]{1,0:T(4,128)}) custom-call(s32[32]{0:T(128)} %heads_ref.1, s32[4]{0:T(128)} %starts_ref.1, bf16[1024,256]{1,0:T(8,128)(2,1)} %x_ref.1, bf16[1024,256]{1,0:T(8,128)(2,1)} %g_ref.1, bf16[1024,128]{1,0:T(8,128)(2,1)} %b_ref.1, ...), custom_call_target="tpu_custom_call" | custom-call | tf_op jit(solution)/shard_map/mixer_backward/pallas_call | solution.py:662
  73.6 3.8 %hand_on.1 = (f32[1024,256]{1,0:T(8,128)}, f32[1024,128]{1,0:T(8,128)}, f32[1024,128]{1,0:T(8,128)}, f32[4,1024]{1,0:T(4,128)}, f32[4,1024]{1,0:T(4,128)}) custom-call(f32[1024,256]{1,0:T(8,128)} %get-tuple-element.9.dx_ref, f32[1024,256]{1,0:T(8,128)} %bitcast.1, f32[4,1024]{1,0:T(4,128)} %get-tuple-element.11.step_ref, f32[4,1024]{1,0:T(4,128)} %get-tuple-element.12.decay_ref), custom_call_target="tpu_custom_call" | custom-call | tf_op jit(solution)/shard_map/hand_on/pallas_call | solution.py:719

commit v4 on v3

--- a/solution.py
+++ b/solution.py
@@ -62,16 +62,25 @@
     ns,
     heads_ref,
     starts_ref,
+    x_hbm,
+    g_hbm,
+    b_hbm,
+    c_hbm,
+    step_ref,
+    decay_ref,
+    dx_hbm,
+    sums_hbm,
+    dstep_ref,
+    ddecay_ref,
     x_ref,
     g_ref,
     b_ref,
     c_ref,
-    step_ref,
-    decay_ref,
+    bt_ref,
+    ct_ref,
     dx_ref,
     sums_ref,
-    dstep_ref,
-    ddecay_ref,
+    local_sems,
     all_ref,
     rows_ref,
     cols_ref,
@@ -133,6 +142,13 @@
         z = lax.rem(z_me + k, zs)
         return z, x_me * 2 * zs + z * 2 + core
 
+    loads = [
+        pltpu.make_async_copy(a, b, local_sems.at[i])
+        for i, (a, b) in enumerate(((x_hbm, x_ref), (g_hbm, g_ref), (b_hbm, b_ref), (c_hbm, c_ref)))
+    ]
+    for load in loads:
+        load.start()
+
     all_ref[head_me, 0:4, :] = step_ref[...]
     all_ref[head_me, 4:8, :] = decay_ref[...]
     barrier = pltpu.get_barrier_semaphore()
@@ -203,9 +219,9 @@
 
 
     def prepare(strand):
-        def chunk(c, carry):
-            base = pl.multiple_of(c * Q, Q)
-            span = pl.ds(base, Q)
+        def chunk(c):
+            base = c * Q
+            span = slice(base, base + Q)
             if strand == 0:
                 s4 = all_ref[head_me, 0:4, span]
                 d4 = all_ref[head_me, 4:8, span]
@@ -243,12 +259,15 @@
             xlo_ref[span, lanes] = xlo
             ghi_ref[span, lanes] = ghi
             glo_ref[span, lanes] = glo
-            bt, ct = b_ref[span, :].T, c_ref[span, :].T
+            if strand == 0:
+                bt_ref[c] = b_ref[span, :].T
+                ct_ref[c] = c_ref[span, :].T
+            bt, ct = bt_ref[c], ct_ref[c]
             ends_ref[c, :, lanes] = dot(bt, xhi) + dot(bt, xlo)
             seeds_ref[c, :, lanes] = dot(ct, ghi) + dot(ct, glo)
-            return carry
-
-        lax.fori_loop(0, chunks, chunk, 0)
+
+        for c in range(chunks):
+            chunk(c)
 
 
     ascending, descending = range(chunks), range(chunks - 1, -1, -1)
@@ -501,6 +520,8 @@
         part[c, :, :, 0:128] = part[c, :, :, 0:128] + db.reshape(nh, part_rows, 128)
         part[c, :, :, 128:256] = part[c, :, :, 128:256] + dc.reshape(nh, part_rows, 128)
 
+    for load in loads:
+        load.wait()
     prepare(0)
     trade(0)
     gathered()
@@ -585,12 +606,17 @@
         total = part[c, head_me]
         for k in range(1, nh):
             total = total + got[c, lax.rem(head_me + k, nh)]
-        sums_ref[c, head_me] = total
+        sums_ref[c] = total
+        own = pltpu.make_async_copy(sums_ref.at[c], sums_hbm.at[c, head_me], local_sems.at[5 + c])
+        own.start()
+        stores.append(own)
         return head_copies(
-            lambda peer: sums_ref.at[c, head_me], sums_ref.at[c, head_me], head_sems.at[2, c], head_sems.at[3, c]
+            lambda peer: sums_ref.at[c], sums_hbm.at[c, head_me], head_sems.at[2, c], head_sems.at[3, c]
         )
 
     lax.fori_loop(0, chunks, across, 0)
+    stores = [pltpu.make_async_copy(dx_ref, dx_hbm, local_sems.at[4])]
+    stores[0].start()
     ny = nh // 2
     y_me, side = lax.rem(head_me, ny), head_me // ny
     x_head = lax.rem(head_me + ny, nh)
@@ -629,14 +655,30 @@
             target[h : h + 1, :] = own_ref[row + h : row + h + 1, :] + back
     for wait in ended:
         wait()
-
-
-def hand_on(dx_ref, sums_ref, step_ref, decay_ref, dx_out, db_out, dc_out, step_out, decay_out):
-    dx_out[...] = dx_ref[...]
-    db_out[...] = sums_ref[:, 0:128]
-    dc_out[...] = sums_ref[:, 128:256]
-    step_out[...] = step_ref[...]
-    decay_out[...] = decay_ref[...]
+    for store in stores:
+        store.wait()
+
+
+def hand_on(dx_ref, sums_ref, step_ref, decay_ref, dx_out, db_out, dc_out, step_out, decay_out, dx, sums, step, decay, sems):
+    pieces = []
+    for c in range(dx_ref.shape[0] // Q):
+        rows = slice(c * Q, (c + 1) * Q)
+        pieces.append((sums_ref.at[rows], sums.at[rows], ((sums.at[rows, 0:128], db_out.at[rows]), (sums.at[rows, 128:256], dc_out.at[rows]))))
+        pieces.append((dx_ref.at[rows], dx.at[rows], ((dx.at[rows], dx_out.at[rows]),)))
+    pieces.append((step_ref, step, ((step, step_out),)))
+    pieces.append((decay_ref, decay, ((decay, decay_out),)))
+    loads = [pltpu.make_async_copy(a, b, sems.at[0, i]) for i, (a, b, _) in enumerate(pieces)]
+    for load in loads:
+        load.start()
+    stores = []
+    for i, (_, _, targets) in enumerate(pieces):
+        loads[i].wait()
+        for k, (a, b) in enumerate(targets):
+            store = pltpu.make_async_copy(a, b, sems.at[1 + k, i])
+            store.start()
+            stores.append(store)
+    for store in stores:
+        store.wait()
 
 
 def on_device(signal, write_keys, read_queries, step_sizes, log_decay, mirror_heads, contig_starts, out_grad):
@@ -648,10 +690,7 @@
     part_rows = Q // nh
     vmem = pl.BlockSpec(memory_space=pltpu.VMEM)
     smem = pl.BlockSpec(memory_space=pltpu.SMEM)
-    across_lanes = pl.BlockSpec((4, Q), lambda i: (0, i))
-
-    def across_rows(width):
-        return pl.BlockSpec((Q, width), lambda i: (i, 0))
+    hbm = pl.BlockSpec(memory_space=pl.ANY)
 
     def shape(*dims, dtype=F32):
         return jax.ShapeDtypeStruct(dims, dtype)
@@ -662,9 +701,18 @@
     dx, sums, dstep, ddecay = pl.pallas_call(
         functools.partial(kernel, nh, ns),
         out_shape=[shape(length, 256), shape(chunks, nh, part_rows, 256), shape(4, length), shape(4, length)],
-        in_specs=[smem] * 2 + [vmem] * 6,
-        out_specs=[vmem] * 4,
+        in_specs=[smem] * 2 + [hbm] * 4 + [vmem] * 2,
+        out_specs=[hbm] * 2 + [vmem] * 2,
         scratch_shapes=[
+            room(length, 256, dtype=BF16),
+            room(length, 256, dtype=BF16),
+            room(length, 128, dtype=BF16),
+            room(length, 128, dtype=BF16),
+            room(chunks, 128, Q, dtype=BF16),
+            room(chunks, 128, Q, dtype=BF16),
+            room(length, 256),
+            room(chunks, part_rows, 256),
+            pltpu.SemaphoreType.DMA((5 + chunks,)),
             room(nh, 8, length),
             room(chunks, 2, 16, Q),
             room(2, length, 16),
@@ -719,9 +767,16 @@
     return pl.pallas_call(
         hand_on,
         out_shape=[shape(length, 256), shape(length, 128), shape(length, 128), shape(4, length), shape(4, length)],
-        grid=(chunks,),
-        in_specs=[across_rows(256)] * 2 + [across_lanes] * 2,
-        out_specs=[across_rows(256), across_rows(128), across_rows(128)] + [across_lanes] * 2,
+        in_specs=[hbm] * 4,
+        out_specs=[hbm] * 5,
+        scratch_shapes=[
+            room(length, 256),
+            room(length, 256),
+            room(4, length),
+            room(4, length),
+            pltpu.SemaphoreType.DMA((3, 2 * chunks + 2)),
+        ],
+        compiler_params=pltpu.CompilerParams(vmem_limit_bytes=VMEM_LIMIT),
         name="hand_on",
     )(dx, sums.reshape(length, 256), dstep, ddecay)
 

time: 77.6 us -> 74.5 us (0.960)
  Pallas kernels: 76.7 us -> 73.7 us
    pallas_call x1, Pallas kernels: 73 us -> 71.2 us  [on_device(): pl.pallas_call(functools.partial(kernel, nh, ns), out_shape=[shape(length...]
    pallas_call x1, Pallas kernels: 3.77 us -> 2.52 us  [on_device(): pl.pallas_call(hand_on, out_shape=[shape(length, 256), shape(length, 128)...]
where the time goes in v4:
time: 74.5 us; the launch traced here: 74.4 us
  Pallas kernels  73.7 us (99%)
    pallas_call x1, Pallas kernels, on_device(): pl.pallas_call(functools.partial(kernel, nh, ns), out_shape=[shape(length...  71.2 us
    pallas_call x1, Pallas kernels, on_device(): pl.pallas_call(hand_on, out_shape=[shape(length, 256), shape(length, 128)...  2.52 us

profile of v4, /device:TPU:1, one launch (start us, length us, event | category | flops | bytes accessed | tf_op | source)
XLA Modules:
  0.0 74.4 jit_solution(18359833053010670523)
XLA Ops:
  0.6 71.2 %mixer_backward.1 = (f32[1024,256]{1,0:T(8,128)}, f32[4,8,32,256]{3,2,1,0:T(8,128)}, f32[4,1024]{1,0:T(4,128)}, f32[4,1024]{1,0:T(4,128)}) custom-call(s32[32]{0:T(128)} %heads_ref.1, s32[4]{0:T(128)} %starts_ref.1, bf16[1024,256]{1,0:T(8,128)(2,1)} %x_hbm.1, bf16[1024,256]{1,0:T(8,128)(2,1)} %g_hbm.1, bf16[1024,128]{1,0:T(8,128)(2,1)} %b_hbm.1, ...), custom_call_target="tpu_custom_call" | custom-call | tf_op jit(solution)/shard_map/mixer_backward/pallas_call | solution.py:701
  71.8 2.5 %hand_on.1 = (f32[1024,256]{1,0:T(8,128)}, f32[1024,128]{1,0:T(8,128)}, f32[1024,128]{1,0:T(8,128)}, f32[4,1024]{1,0:T(4,128)}, f32[4,1024]{1,0:T(4,128)}) custom-call(f32[1024,256]{1,0:T(8,128)} %get-tuple-element.9.dx_ref, f32[1024,256]{1,0:T(8,128)} %bitcast.1, f32[4,1024]{1,0:T(4,128)} %get-tuple-element.11.step_ref, f32[4,1024]{1,0:T(4,128)} %get-tuple-element.12.decay_ref), custom_call_target="tpu_custom_call" | custom-call | tf_op jit(solution)/shard_map/hand_on/pallas_call | solution.py:767

commit v5 on v4

--- a/solution.py
+++ b/solution.py
@@ -84,13 +84,10 @@
     all_ref,
     rows_ref,
     cols_ref,
-    xhi_ref,
-    xlo_ref,
-    ghi_ref,
-    glo_ref,
+    hi_ref,
+    lo_ref,
     el_ref,
-    ends_ref,
-    seeds_ref,
+    terms_ref,
     gain_ref,
     pair_out,
     pair_in,
@@ -102,8 +99,7 @@
     back_in,
     next_out,
     entering,
-    states,
-    adjoints,
+    meet,
     gm,
     pt,
     whi,
@@ -255,16 +251,16 @@
             el_ref[span, lanes] = wide[:, 0:256]
             xhi, xlo = split2(x_ref[span, :].astype(F32) * wide[:, 0:256])
             ghi, glo = split2(g_ref[span, :].astype(F32) * wide[:, 256:512])
-            xhi_ref[span, lanes] = xhi
-            xlo_ref[span, lanes] = xlo
-            ghi_ref[span, lanes] = ghi
-            glo_ref[span, lanes] = glo
+            hi_ref[0, span, lanes] = xhi
+            lo_ref[0, span, lanes] = xlo
+            hi_ref[1, span, lanes] = ghi
+            lo_ref[1, span, lanes] = glo
             if strand == 0:
                 bt_ref[c] = b_ref[span, :].T
                 ct_ref[c] = c_ref[span, :].T
             bt, ct = bt_ref[c], ct_ref[c]
-            ends_ref[c, :, lanes] = dot(bt, xhi) + dot(bt, xlo)
-            seeds_ref[c, :, lanes] = dot(ct, ghi) + dot(ct, glo)
+            terms_ref[1, c, :, lanes] = dot(bt, xhi) + dot(bt, xlo)
+            terms_ref[0, c, :, lanes] = dot(ct, ghi) + dot(ct, glo)
 
         for c in range(chunks):
             chunk(c)
@@ -273,15 +269,15 @@
     ascending, descending = range(chunks), range(chunks - 1, -1, -1)
     way = (ascending, descending)
 
-    def terms_of(strand, d):
-        return (ends_ref, seeds_ref)[(strand + d) % 2]
+    def kind(strand, d):
+        return d if strand else 1 - d
 
     def fold(strand):
         lanes = STRANDS[strand]
         for d in range(2):
             run = None
             for c in way[d]:
-                term = terms_of(strand, d)[c, :, lanes]
+                term = terms_ref[kind(strand, d), c, :, lanes]
                 run = term if run is None else run * gain_ref[c, 0:1, lanes] + term
             for k in range(2):
                 pair_out[strand, d, k * 128 : (k + 1) * 128] = run[:, k * 128 : (k + 1) * 128]
@@ -295,11 +291,7 @@
 
     half_mask = [jnp.where(iota((1, 128), 1) // 64 == k, 1.0, 0.0).astype(BF16) for k in range(2)]
     zero_row = jnp.zeros((8, 128), F32)
-    part_rows = Q // nh
-
-    def put_part(c, lanes, value):
-        part[c, :, :, lanes] = value.reshape(nh, part_rows, 128)
-
+    part_rows = length // nh
     kept_sums = {}
 
     def inside(c, i):
@@ -400,9 +392,9 @@
                 term = dot(whi[h], masked) + dot(wlo[h], masked)
                 total = term if total is None else total + term
             dx_ref[span, k * 128 : (k + 1) * 128] = total
-        put_part(c, slice(0, 128), dot(dghi[...], cc) + dot(dglo[...], cc))
+        part[0, span, :] = dot(dghi[...], cc) + dot(dglo[...], cc)
         dgt_hi, dgt_lo = dghi[...].T, dglo[...].T
-        put_part(c, slice(128, 256), dot(dgt_hi, bc) + dot(dgt_lo, bc))
+        part[1, span, :] = dot(dgt_hi, bc) + dot(dgt_lo, bc)
 
 
     other = 1 - core
@@ -496,29 +488,31 @@
         copy.start()
         waits["pass", strand] = copy.wait
 
-    def enter_chunks(strand):
-        waits["pass", strand]()
+    def enter_chunks(strand, d):
         lanes = STRANDS[strand]
-        for d in range(2):
-            terms = terms_of(strand, d)
-            target = states if terms is ends_ref else adjoints
-            run = jnp.concatenate([entering[strand, d, k * 128 : (k + 1) * 128] for k in range(2)], axis=1)
-            for c in way[d]:
-                target[c, :, lanes] = run
-                run = run * gain_ref[c, 0:1, lanes] + terms[c, :, lanes]
-            if target is states:
-                target[chunks, :, lanes] = run
-
-    def cross(c, strand):
-        span = slice(c * Q, (c + 1) * Q)
+        w = kind(strand, d)
+        run = jnp.concatenate([entering[strand, d, k * 128 : (k + 1) * 128] for k in range(2)], axis=1)
+        for i in range(chunks):
+            c = i + d * (chunks - 1 - 2 * i)
+            meet[w, c, :, lanes] = run
+            run = run * gain_ref[c, 0:1, lanes] + terms_ref[w, c, :, lanes]
+        meet[w, chunks, :, lanes] = run
+
+    def cross(strand, w):
         lanes = STRANDS[strand]
-        state_hi, state_lo = split2(states[c, :, lanes])
-        adj_hi, adj_lo = split2(adjoints[c, :, lanes])
-        xhi, xlo, ghi, glo = xhi_ref[span, lanes], xlo_ref[span, lanes], ghi_ref[span, lanes], glo_ref[span, lanes]
-        db = dot_nt(xhi, adj_hi) + dot_nt(xlo, adj_hi) + dot_nt(xhi, adj_lo)
-        dc = dot_nt(ghi, state_hi) + dot_nt(glo, state_hi) + dot_nt(ghi, state_lo)
-        part[c, :, :, 0:128] = part[c, :, :, 0:128] + db.reshape(nh, part_rows, 128)
-        part[c, :, :, 128:256] = part[c, :, :, 128:256] + dc.reshape(nh, part_rows, 128)
+        for c in range(chunks):
+            span = slice(c * Q, (c + 1) * Q)
+            m_hi, m_lo = split2(meet[w, c, :, lanes])
+            hi, lo = hi_ref[w, span, lanes], lo_ref[w, span, lanes]
+            part[w, span, :] = part[w, span, :] + (dot_nt(hi, m_hi) + dot_nt(lo, m_hi) + dot_nt(hi, m_lo))
+
+    def share(w, n):
+        return head_copies(
+            lambda peer: part.at[w, pl.ds(peer * part_rows, part_rows)],
+            got.at[w, head_me],
+            head_sems.at[0, n],
+            head_sems.at[1, n],
+        )
 
     for load in loads:
         load.wait()
@@ -532,18 +526,24 @@
     inside(0, 0)
     spread_chip(1)
     inside(0, 1)
-    send_back(0)
     inside(1, 0)
     inside(1, 1)
     scan_half(1)
+    send_back(0)
     inside(2, 0)
-    pass_on(0)
     inside(2, 1)
     send_back(1)
     inside(3, 0)
+    pass_on(0)
     inside(3, 1)
-    enter_chunks(0)
+    waits["pass", 0]()
+    for d in range(2):
+        enter_chunks(0, d)
+        cross(0, kind(0, d))
     pass_on(1)
+    enter_chunks(1, core)
+    cross(1, core)
+    sent = [share(core, 0)]
 
     pick = jnp.where(iota((8, 512), 0) == iota((8, 512), 1) // 64, 1.0, 0.0)
     pick_bf = pick.astype(BF16)
@@ -560,37 +560,29 @@
         return carry
 
     lax.fori_loop(0, chunks, same_place, 0)
-    for c in range(chunks):
-        cross(c, 0)
-    enter_chunks(1)
-
-    sent = []
-    for c in range(chunks):
-        cross(c, 1)
-        sent.append(
-            head_copies(
-                lambda peer, c=c: part.at[c, peer], got.at[c, head_me], head_sems.at[0, c], head_sems.at[1, c]
-            )
-        )
+    waits["pass", 1]()
+    enter_chunks(1, other)
+    cross(1, other)
+    sent.append(share(other, 1))
 
     def across(c, carry):
         span = pl.ds(pl.multiple_of(c * Q, Q), Q)
-        state_hi, state_lo = split2(states[c])
-        adj_hi, adj_lo = split2(adjoints[c])
+        state_hi, state_lo = split2(meet[1, c])
+        adj_hi, adj_lo = split2(meet[0, c])
         bc, cc = b_ref[span, :], c_ref[span, :]
         v = dot(bc, adj_hi) + dot(bc, adj_lo)
         y = dot(cc, state_hi) + dot(cc, state_lo)
         scaled = el_ref[span, :] * v
         dx_ref[span, :] = dx_ref[span, :] + scaled[:, FRONT] + scaled[:, MIRROR]
-        x_prod = split2((xhi_ref[span, :].astype(F32) + xlo_ref[span, :].astype(F32)) * v)
-        g_prod = split2((ghi_ref[span, :].astype(F32) + glo_ref[span, :].astype(F32)) * y)
+        x_prod = split2((hi_ref[0, span, :].astype(F32) + lo_ref[0, span, :].astype(F32)) * v)
+        g_prod = split2((hi_ref[1, span, :].astype(F32) + lo_ref[1, span, :].astype(F32)) * y)
         col8 = col_keep[c] + dot_nt(pick_bf, x_prod[0]) + dot_nt(pick_bf, x_prod[1])
         row8 = row_keep[c] + dot_nt(pick_bf, g_prod[0]) + dot_nt(pick_bf, g_prod[1])
         s8 = jnp.concatenate([rows_ref[c, 0, 12:16, :], rows_ref[c, 1, 12:16, :]], axis=0)
         step8 = col8 / s8 + other_ref[:, span]
-        flow_f = jnp.sum(states[c + 1, :, FRONT] * adjoints[c, :, FRONT], axis=0, keepdims=True)
+        flow_f = jnp.sum(meet[1, c + 1, :, FRONT] * meet[0, c, :, FRONT], axis=0, keepdims=True)
         under = lax.rem(c + chunks, chunks + 1)
-        flow_m = jnp.sum(states[under, :, MIRROR] * adjoints[c, :, MIRROR], axis=0, keepdims=True)
+        flow_m = jnp.sum(meet[1, under, :, MIRROR] * meet[0, c, :, MIRROR], axis=0, keepdims=True)
         flow8 = jnp.sum(pick * jnp.concatenate([flow_f, flow_m], axis=1), axis=1, keepdims=True)
         diff = split3(row8 - col8)
         front8 = iota((8, Q), 0) < 4
@@ -601,17 +593,19 @@
         other_ref[4:8, span] = decay8[4:8]
         return carry
 
-    def add_up(c):
-        sent[c]()
-        total = part[c, head_me]
+    own_rows = pl.ds(head_me * part_rows, part_rows)
+
+    def add_up(w, n):
+        sent[n]()
+        total = part[w, own_rows, :]
         for k in range(1, nh):
-            total = total + got[c, lax.rem(head_me + k, nh)]
-        sums_ref[c] = total
-        own = pltpu.make_async_copy(sums_ref.at[c], sums_hbm.at[c, head_me], local_sems.at[5 + c])
+            total = total + got[w, lax.rem(head_me + k, nh)]
+        sums_ref[w] = total
+        own = pltpu.make_async_copy(sums_ref.at[w], sums_hbm.at[w, own_rows], local_sems.at[5 + n])
         own.start()
         stores.append(own)
         return head_copies(
-            lambda peer: sums_ref.at[c], sums_hbm.at[c, head_me], head_sems.at[2, c], head_sems.at[3, c]
+            lambda peer: sums_ref.at[w], sums_hbm.at[w, own_rows], head_sems.at[2, n], head_sems.at[3, n]
         )
 
     lax.fori_loop(0, chunks, across, 0)
@@ -637,7 +631,7 @@
     def row_of(place, row):
         return others[lax.rem(place // 4, ny), pl.ds(lax.rem(place, 4) + row, 1), :]
 
-    ended = [add_up(c) for c in range(chunks // 2)]
+    ended = [add_up(core, 0)]
     shared()
     for h in range(4):
         place = find(x_head * 4 + h)
@@ -645,7 +639,7 @@
         far_out[4 + h : 5 + h, :] = row_of(place, 4)
     far = remote(far_out, far_in, other_sems.at[0, 0], other_sems.at[1, 0], "head", x_head)
     far.start()
-    ended += [add_up(c) for c in range(chunks // 2, chunks)]
+    ended.append(add_up(other, 1))
     far.wait()
     for h in range(4):
         place = find(head_me * 4 + h)
@@ -663,20 +657,19 @@
     pieces = []
     for c in range(dx_ref.shape[0] // Q):
         rows = slice(c * Q, (c + 1) * Q)
-        pieces.append((sums_ref.at[rows], sums.at[rows], ((sums.at[rows, 0:128], db_out.at[rows]), (sums.at[rows, 128:256], dc_out.at[rows]))))
-        pieces.append((dx_ref.at[rows], dx.at[rows], ((dx.at[rows], dx_out.at[rows]),)))
-    pieces.append((step_ref, step, ((step, step_out),)))
-    pieces.append((decay_ref, decay, ((decay, decay_out),)))
+        for w, out in enumerate((db_out, dc_out)):
+            pieces.append((sums_ref.at[w, rows], sums.at[w, rows], out.at[rows]))
+        pieces.append((dx_ref.at[rows], dx.at[rows], dx_out.at[rows]))
+    pieces.append((step_ref, step, step_out))
+    pieces.append((decay_ref, decay, decay_out))
     loads = [pltpu.make_async_copy(a, b, sems.at[0, i]) for i, (a, b, _) in enumerate(pieces)]
     for load in loads:
         load.start()
     stores = []
-    for i, (_, _, targets) in enumerate(pieces):
+    for i, (_, a, b) in enumerate(pieces):
         loads[i].wait()
-        for k, (a, b) in enumerate(targets):
-            store = pltpu.make_async_copy(a, b, sems.at[1 + k, i])
-            store.start()
-            stores.append(store)
+        stores.append(pltpu.make_async_copy(a, b, sems.at[1, i]))
+        stores[-1].start()
     for store in stores:
         store.wait()
 
@@ -687,7 +680,7 @@
     chunks = length // Q
     zs = ns // 4
     slice_rows = 256 // zs
-    part_rows = Q // nh
+    part_rows = length // nh
     vmem = pl.BlockSpec(memory_space=pltpu.VMEM)
     smem = pl.BlockSpec(memory_space=pltpu.SMEM)
     hbm = pl.BlockSpec(memory_space=pl.ANY)
@@ -700,7 +693,7 @@
 
     dx, sums, dstep, ddecay = pl.pallas_call(
         functools.partial(kernel, nh, ns),
-        out_shape=[shape(length, 256), shape(chunks, nh, part_rows, 256), shape(4, length), shape(4, length)],
+        out_shape=[shape(length, 256), shape(2, length, 128), shape(4, length), shape(4, length)],
         in_specs=[smem] * 2 + [hbm] * 4 + [vmem] * 2,
         out_specs=[hbm] * 2 + [vmem] * 2,
         scratch_shapes=[
@@ -711,18 +704,15 @@
             room(chunks, 128, Q, dtype=BF16),
             room(chunks, 128, Q, dtype=BF16),
             room(length, 256),
-            room(chunks, part_rows, 256),
-            pltpu.SemaphoreType.DMA((5 + chunks,)),
+            room(2, part_rows, 128),
+            pltpu.SemaphoreType.DMA((7,)),
             room(nh, 8, length),
             room(chunks, 2, 16, Q),
             room(2, length, 16),
-            room(length, 512, dtype=BF16),
-            room(length, 512, dtype=BF16),
-            room(length, 512, dtype=BF16),
-            room(length, 512, dtype=BF16),
+            room(2, length, 512, dtype=BF16),
+            room(2, length, 512, dtype=BF16),
             room(length, 512),
-            room(chunks, 128, 512),
-            room(chunks, 128, 512),
+            room(2, chunks, 128, 512),
             room(chunks, 8, 512),
             room(2, 2, 272, 128),
             room(2, 272, 128),
@@ -734,8 +724,7 @@
             room(2, zs, slice_rows, 128),
             room(2, 256, 128),
             room(2, 2, 256, 128),
-            room(chunks + 1, 128, 512),
-            room(chunks, 128, 512),
+            room(2, chunks + 1, 128, 512),
             room(Q, Q),
             room(4, Q, Q),
             room(4, Q, Q, dtype=BF16),
@@ -745,8 +734,8 @@
             room(Q, 128),
             room(chunks, 8, Q),
             room(chunks, 8, Q),
-            room(chunks, nh, part_rows, 256),
-            room(chunks, nh, part_rows, 256),
+            room(2, length, 128),
+            room(2, nh, part_rows, 128),
             room(8, length),
             room(8, length),
             room(nh // 2, 8, length),
@@ -755,7 +744,7 @@
             pltpu.SemaphoreType.DMA((2, nh)),
             pltpu.SemaphoreType.DMA((2, 6)),
             pltpu.SemaphoreType.DMA((2, 4, zs)),
-            pltpu.SemaphoreType.DMA((4, chunks, nh)),
+            pltpu.SemaphoreType.DMA((4, 2, nh)),
             pltpu.SemaphoreType.DMA((2, nh)),
         ],
         compiler_params=pltpu.CompilerParams(
@@ -771,14 +760,14 @@
         out_specs=[hbm] * 5,
         scratch_shapes=[
             room(length, 256),
-            room(length, 256),
+            room(2, length, 128),
             room(4, length),
             room(4, length),
-            pltpu.SemaphoreType.DMA((3, 2 * chunks + 2)),
+            pltpu.SemaphoreType.DMA((2, 3 * chunks + 2)),
         ],
         compiler_params=pltpu.CompilerParams(vmem_limit_bytes=VMEM_LIMIT),
         name="hand_on",
-    )(dx, sums.reshape(length, 256), dstep, ddecay)
+    )(dx, sums, dstep, ddecay)
 
 
 def solution(mesh):

time: 74.5 us -> 71.2 us (0.956)
  Pallas kernels: 73.7 us -> 70.4 us
    pallas_call x1, Pallas kernels: 71.2 us -> 67.8 us  [on_device(): pl.pallas_call(functools.partial(kernel, nh, ns), out_shape=[shape(length...]
where the time goes in v5:
time: 71.2 us; the launch traced here: 71 us
  Pallas kernels  70.4 us (99%)
    pallas_call x1, Pallas kernels, on_device(): pl.pallas_call(functools.partial(kernel, nh, ns), out_shape=[shape(length...  67.8 us
    pallas_call x1, Pallas kernels, on_device(): pl.pallas_call(hand_on, out_shape=[shape(length, 256), shape(length, 128)...  2.55 us

profile of v5, /device:TPU:1, one launch (start us, length us, event | category | flops | bytes accessed | tf_op | source)
XLA Modules:
  0.0 71.0 jit_solution(9137489323802029703)
XLA Ops:
  0.6 67.8 %mixer_backward.1 = (f32[1024,256]{1,0:T(8,128)}, f32[2,1024,128]{2,1,0:T(8,128)}, f32[4,1024]{1,0:T(4,128)}, f32[4,1024]{1,0:T(4,128)}) custom-call(s32[32]{0:T(128)} %heads_ref.1, s32[4]{0:T(128)} %starts_ref.1, bf16[1024,256]{1,0:T(8,128)(2,1)} %x_hbm.1, bf16[1024,256]{1,0:T(8,128)(2,1)} %g_hbm.1, bf16[1024,128]{1,0:T(8,128)(2,1)} %b_hbm.1, ...), custom_call_target="tpu_custom_call" | custom-call | tf_op jit(solution)/shard_map/mixer_backward/pallas_call | solution.py:694
  68.4 2.6 %hand_on.1 = (f32[1024,256]{1,0:T(8,128)}, f32[1024,128]{1,0:T(8,128)}, f32[1024,128]{1,0:T(8,128)}, f32[4,1024]{1,0:T(4,128)}, f32[4,1024]{1,0:T(4,128)}) custom-call(f32[1024,256]{1,0:T(8,128)} %get-tuple-element.9.dx_ref, f32[2,1024,128]{2,1,0:T(8,128)} %get-tuple-element.10.sums_ref, f32[4,1024]{1,0:T(4,128)} %get-tuple-element.11.step_ref, ...), custom_call_target="tpu_custom_call" | custom-call | tf_op jit(solution)/shard_map/hand_on/pallas_call | solution.py:756

commit v6 on v5

--- a/solution.py
+++ b/solution.py
@@ -195,7 +195,8 @@
 
     def z_copies(source, target, send, recv):
         def copy(k):
-            z, peer = z_peer(k)
+            step = (k // 2) * (2 * lax.rem(k, 2) - 1)
+            z, peer = z_peer(zs // 2 + step)
             return remote(source(z), target, send.at[k], recv.at[k], "seq", peer)
 
         return every(zs, copy)

time: 71.2 us -> 69.8 us (0.980)
  Pallas kernels: 70.4 us -> 69 us
    pallas_call x1, Pallas kernels: 67.8 us -> 66.5 us  [on_device(): pl.pallas_call(functools.partial(kernel, nh, ns), out_shape=[shape(length...]
where the time goes in v6:
time: 69.8 us; the launch traced here: 69.7 us
  Pallas kernels  69 us (99%)
    pallas_call x1, Pallas kernels, on_device(): pl.pallas_call(functools.partial(kernel, nh, ns), out_shape=[shape(length...  66.5 us
    pallas_call x1, Pallas kernels, on_device(): pl.pallas_call(hand_on, out_shape=[shape(length, 256), shape(length, 128)...  2.55 us

profile of v6, /device:TPU:1, one launch (start us, length us, event | category | flops | bytes accessed | tf_op | source)
XLA Modules:
  0.0 69.7 jit_solution(11352534133831780927)
XLA Ops:
  0.6 66.5 %mixer_backward.1 = (f32[1024,256]{1,0:T(8,128)}, f32[2,1024,128]{2,1,0:T(8,128)}, f32[4,1024]{1,0:T(4,128)}, f32[4,1024]{1,0:T(4,128)}) custom-call(s32[32]{0:T(128)} %heads_ref.1, s32[4]{0:T(128)} %starts_ref.1, bf16[1024,256]{1,0:T(8,128)(2,1)} %x_hbm.1, bf16[1024,256]{1,0:T(8,128)(2,1)} %g_hbm.1, bf16[1024,128]{1,0:T(8,128)(2,1)} %b_hbm.1, ...), custom_call_target="tpu_custom_call" | custom-call | tf_op jit(solution)/shard_map/mixer_backward/pallas_call | solution.py:695
  67.1 2.6 %hand_on.1 = (f32[1024,256]{1,0:T(8,128)}, f32[1024,128]{1,0:T(8,128)}, f32[1024,128]{1,0:T(8,128)}, f32[4,1024]{1,0:T(4,128)}, f32[4,1024]{1,0:T(4,128)}) custom-call(f32[1024,256]{1,0:T(8,128)} %get-tuple-element.9.dx_ref, f32[2,1024,128]{2,1,0:T(8,128)} %get-tuple-element.10.sums_ref, f32[4,1024]{1,0:T(4,128)} %get-tuple-element.11.step_ref, ...), custom_call_target="tpu_custom_call" | custom-call | tf_op jit(solution)/shard_map/hand_on/pallas_call | solution.py:757

commit v7 on v6

--- a/solution.py
+++ b/solution.py
@@ -560,11 +560,11 @@
         other_ref[:, span] = score8 * pair8
         return carry
 
-    lax.fori_loop(0, chunks, same_place, 0)
     waits["pass", 1]()
     enter_chunks(1, other)
     cross(1, other)
     sent.append(share(other, 1))
+    lax.fori_loop(0, chunks, same_place, 0)
 
     def across(c, carry):
         span = pl.ds(pl.multiple_of(c * Q, Q), Q)
@@ -609,7 +609,7 @@
             lambda peer: sums_ref.at[w], sums_hbm.at[w, own_rows], head_sems.at[2, n], head_sems.at[3, n]
         )
 
-    lax.fori_loop(0, chunks, across, 0)
+    lax.fori_loop(0, chunks, across, 0, unroll=True)
     stores = [pltpu.make_async_copy(dx_ref, dx_hbm, local_sems.at[4])]
     stores[0].start()
     ny = nh // 2

time: 69.8 us -> 69.9 us (level)
  no operation moved by 1% of the time
where the time goes in v7:
time: 69.9 us; the launch traced here: 69.7 us
  Pallas kernels  68.9 us (99%)
  between operations  0.8 us (1%)
    pallas_call x1, Pallas kernels, on_device(): pl.pallas_call(functools.partial(kernel, nh, ns), out_shape=[shape(length...  66.4 us
    pallas_call x1, Pallas kernels, on_device(): pl.pallas_call(hand_on, out_shape=[shape(length, 256), shape(length, 128)...  2.55 us

profile of v7, /device:TPU:1, one launch (start us, length us, event | category | flops | bytes accessed | tf_op | source)
XLA Modules:
  0.0 69.7 jit_solution(2670622458059741481)
XLA Ops:
  0.6 66.4 %mixer_backward.1 = (f32[1024,256]{1,0:T(8,128)}, f32[2,1024,128]{2,1,0:T(8,128)}, f32[4,1024]{1,0:T(4,128)}, f32[4,1024]{1,0:T(4,128)}) custom-call(s32[32]{0:T(128)} %heads_ref.1, s32[4]{0:T(128)} %starts_ref.1, bf16[1024,256]{1,0:T(8,128)(2,1)} %x_hbm.1, bf16[1024,256]{1,0:T(8,128)(2,1)} %g_hbm.1, bf16[1024,128]{1,0:T(8,128)(2,1)} %b_hbm.1, ...), custom_call_target="tpu_custom_call" | custom-call | tf_op jit(solution)/shard_map/mixer_backward/pallas_call | solution.py:695
  67.0 2.6 %hand_on.1 = (f32[1024,256]{1,0:T(8,128)}, f32[1024,128]{1,0:T(8,128)}, f32[1024,128]{1,0:T(8,128)}, f32[4,1024]{1,0:T(4,128)}, f32[4,1024]{1,0:T(4,128)}) custom-call(f32[1024,256]{1,0:T(8,128)} %get-tuple-element.9.dx_ref, f32[2,1024,128]{2,1,0:T(8,128)} %get-tuple-element.10.sums_ref, f32[4,1024]{1,0:T(4,128)} %get-tuple-element.11.step_ref, ...), custom_call_target="tpu_custom_call" | custom-call | tf_op jit(solution)/shard_map/hand_on/pallas_call | solution.py:757
